TPU v7x, 256 devices: a whole 4x4x8 slice. The times are simulated.
256 devices in a mesh: az: 32 (over z_lo, x, core), rad: 8 (over z_hi, y).
Axes of the slice: x: 4, y: 4, z: 8 (z_hi: 2, z_lo: 4; z = z_hi * 4 + z_lo), core: 2. Of those that a mesh axis runs over, the one named last changes fastest.
Arguments:
- conserved: float32 [8, 16, 64, 4096], P(None, None, 'rad', 'az'), as said below
- shear_shift: int32 [2], replicated, may hold values from 0 to 4095
Outputs:
- tendency: float32 [8, 16, 64, 4096], P(None, None, 'rad', 'az')
Inputs may be any that keep to these rules, and one draw needn't show every extreme that they name: `conserved`: every cell has positive density and positive pressure.
All inputs are finite; a program needn't handle non-finite values.
Results may differ from a plain program's by a relative error of at most 0.0003.
Values sent between devices are 32-bit elements; how exact they have to be, the bound alone decides.
A program may use at most 64 MiB of HBM per device.

v0:
```python
import jax
import jax.numpy as jnp
from jax import lax
from jax.sharding import PartitionSpec as P

adiabatic = 5.0 / 3.0
time_step = 0.02
shear_jump = 0.5


def padded_2(value, sides, width):
    for axis, dim in sides:
        peers, length = (lax.axis_size(axis), value.shape[dim])
        up = [(i, (i + 1) % peers) for i in range(peers)]
        down = [(j, i) for i, j in up]
        last = lax.slice_in_dim(value, length - width, length, axis=dim)
        first = lax.slice_in_dim(value, 0, width, axis=dim)
        before = lax.ppermute(last, axis, up)
        after = lax.ppermute(first, axis, down)
        value = jnp.concatenate([before, value, after], axis=dim)
    return value


def shifted_2(value, axis, steps):
    count = lax.axis_size(axis)
    pairs = [(source, (source + steps) % count) for source in range(count)]
    return lax.ppermute(value, axis, pairs)


def primitive_of(conserved):
    density = conserved[0]
    velocity = conserved[1:4] / density
    magnetic = conserved[5:8]
    pressure = (adiabatic - 1.0) * (
        conserved[4]
        - 0.5 * density * jnp.sum(velocity * velocity, axis=0)
        - 0.5 * jnp.sum(magnetic * magnetic, axis=0)
    )
    return jnp.concatenate([density[None], velocity, pressure[None], magnetic], axis=0)


def flux_of(primitive, normal):
    density = primitive[0]
    velocity = primitive[1:4]
    pressure = primitive[4]
    magnetic = primitive[5:8]
    normal_vel = velocity[normal]
    normal_mag = magnetic[normal]
    mag_square = jnp.sum(magnetic * magnetic, axis=0)
    total_pres = pressure + 0.5 * mag_square
    energy = (
        pressure / (adiabatic - 1.0)
        + 0.5 * density * jnp.sum(velocity * velocity, axis=0)
        + 0.5 * mag_square
    )
    conserved = jnp.concatenate([density[None], density * velocity, energy[None], magnetic], axis=0)
    selector = (
        (jnp.arange(3) == normal)
        .astype(primitive.dtype)
        .reshape((3,) + (1,) * (primitive.ndim - 1))
    )
    momentum = density * velocity * normal_vel - magnetic * normal_mag + selector * total_pres
    induction = magnetic * normal_vel - velocity * normal_mag
    power = (energy + total_pres) * normal_vel - normal_mag * jnp.sum(velocity * magnetic, axis=0)
    face_flux = jnp.concatenate(
        [(density * normal_vel)[None], momentum, power[None], induction], axis=0
    )
    signal_speed = jnp.abs(normal_vel) + jnp.sqrt((adiabatic * pressure + mag_square) / density)
    return (conserved, face_flux, signal_speed)


def face_difference(padded, along, normal):
    length = padded.shape[along]
    cells = length - 4
    centre = lax.slice_in_dim(padded, 1, length - 1, axis=along)
    back_diff = centre - lax.slice_in_dim(padded, 0, length - 2, axis=along)
    fore_diff = lax.slice_in_dim(padded, 2, length, axis=along) - centre
    slopes = (
        0.5
        * (jnp.sign(back_diff) + jnp.sign(fore_diff))
        * jnp.minimum(jnp.abs(back_diff), jnp.abs(fore_diff))
    )
    left_state = lax.slice_in_dim(centre + 0.5 * slopes, 0, cells + 1, axis=along)
    right_state = lax.slice_in_dim(centre - 0.5 * slopes, 1, cells + 2, axis=along)
    left_cons, left_flux, left_speed = flux_of(left_state, normal)
    right_cons, right_flux, right_speed = flux_of(right_state, normal)
    face_flux = 0.5 * (left_flux + right_flux) - 0.5 * jnp.maximum(left_speed, right_speed) * (
        right_cons - left_cons
    )
    return lax.slice_in_dim(face_flux, 1, cells + 1, axis=along) - lax.slice_in_dim(
        face_flux, 0, cells, axis=along
    )


def tendency_of(x_padded, y_padded):
    core = x_padded[:, :, 2:-2, :]
    z_padded = jnp.concatenate([core[:, -2:], core, core[:, :2]], axis=1)
    return -(
        face_difference(x_padded, 2, 0)
        + face_difference(y_padded, 3, 1)
        + face_difference(z_padded, 1, 2)
    )


def shards(conserved, shear_shift):
    az_count = lax.axis_size("az")
    rad_count = lax.axis_size("rad")
    az_place = lax.axis_index("az")
    rad_place = lax.axis_index("rad")
    columns = conserved.shape[3]
    total_cols = columns * az_count
    kick = shear_jump * (jnp.arange(8) == 2).astype(jnp.float32)[:, None, None, None]

    def section(primitive, offset):
        y_padded = padded_2(primitive, (("az", 3),), 2)
        strips = jnp.stack([primitive[:, :, -2:, :], primitive[:, :, :2, :]])
        amounts = jnp.stack([offset, (total_cols - offset) % total_cols])
        gathered = lax.all_gather(strips, "az", axis=4, tiled=True)
        doubled = jnp.concatenate([gathered, gathered], axis=4)
        begins = (az_place * columns + amounts) % total_cols
        shifted = jnp.stack(
            [
                lax.dynamic_slice_in_dim(doubled[0], begins[0], columns, axis=3),
                lax.dynamic_slice_in_dim(doubled[1], begins[1], columns, axis=3),
            ]
        )
        send_up = jnp.where(rad_place == rad_count - 1, shifted[0] + kick, strips[0])
        send_down = jnp.where(rad_place == 0, shifted[1] - kick, strips[1])
        low_rows = shifted_2(send_up, "rad", 1)
        high_rows = shifted_2(send_down, "rad", -1)
        x_padded = jnp.concatenate([low_rows, primitive, high_rows], axis=2)
        return tendency_of(x_padded, y_padded)

    first = section(primitive_of(conserved), shear_shift[0])
    midpoint = conserved + time_step * first
    second = section(primitive_of(midpoint), shear_shift[1])
    return 0.5 * (first + second)


def solution(mesh):
    return jax.shard_map(
        shards,
        mesh=mesh,
        in_specs=(P(None, None, "rad", "az"), P()),
        out_specs=P(None, None, "rad", "az"),
        check_vma=False,
    )
```

profile of v0, /device:TPU:24, one launch (start us, length us, event | category | flops | bytes accessed | tf_op | source)
XLA Modules:
  0.0 259.2 jit_solution(17469210797384590116)
XLA Ops:
  6.5 0.8 fusion.192
  7.4 1.1 multiply_reduce_fusion.39
  8.5 0.9 fusion.138
  9.5 0.8 pad_maximum_fusion.32
  10.4 1.0 fusion.191
  11.4 6.3 %collective-permute-start.3 = (f32[8,16,8,2]{3,2,1,0:T(8,128)S(1)}, f32[8,16,8,2]{3,2,1,0:T(8,128)S(1)}, u32[]{:S(2)}, u32[]{:S(2)}) collective-permute-start(f32[8,16,8,2]{3,2,1,0:T(8,128)S(1)} %get-tuple-element.256), channel_id=1, source_target_pairs={{8,0},{16,8},{24,16},{32,24},{40,32},{48,40},{56,48},{64,56},{72,6... | collective-permute-start | bytes 24584 | tf_op jit(solution)/shard_map/ppermute | solution.py:19
  17.7 1.3 fusion.194
  20.2 1.3 and_select_fusion
  21.5 0.6 fusion.195
  22.1 0.3 fusion.102
  22.4 0.3 fusion.103
  27.0 1.1 fusion.158
  28.1 1.1 fusion.159
  29.2 0.3 multiply_reduce_fusion.14
  29.5 1.0 fusion.184
  30.5 1.0 fusion.183
  31.5 1.5 multiply_add_fusion.5
  33.0 67.5 %all-gather.3.cloned.1.call-done = f32[2,8,16,2,4096]{4,3,2,1,0:T(2,128)} async-done(((f32[2,8,16,2,128]{4,3,2,1,0:T(2,128)}), f32[2,8,16,2,4096]{4,3,2,1,0:T(2,128)}) %all-gather.3.cloned.1.call-update) | async-done | bytes 8388624 | tf_op jit(solution)/shard_map/all_gather | solution.py:118
  100.4 4.9 %constant_dynamic-update-slice_fusion.1 = f32[2,8,16,2,8192]{4,3,2,1,0:T(2,128)S(1)} fusion(f32[2,8,16,2,4096]{4,3,2,1,0:T(2,128)} %all-gather.3.cloned.1.call-done), kind=kLoop, calls=%fused_computation.406 | loop fusion | bytes 16777216
  105.4 1.0 copy-done
  106.3 1.2 constant_dynamic-update-slice_fusion
  107.7 1.8 fusion.176
  109.5 0.4 fusion.93
  109.9 4.7 %collective-permute-start = (f32[8,16,2,128]{3,2,1,0:T(2,128)S(1)}, f32[8,16,2,128]{3,2,1,0:T(2,128)S(1)}, u32[]{:S(2)}, u32[]{:S(2)}) collective-permute-start(f32[8,16,2,128]{3,2,1,0:T(2,128)S(1)} %get-tuple-element.239), channel_id=1, source_target_pairs={{0,1},{1,2},{2,3},{3,4},{4,5},{5,6},{6,7},{7,0},{8,9},{9,10},{10,1... | collective-permute-start | bytes 393224 | tf_op jit(solution)/shard_map/ppermute | solution.py:27
  114.8 0.4 fusion.4
  115.2 3.3 %collective-permute-done = f32[8,16,2,128]{3,2,1,0:T(2,128)S(1)} collective-permute-done((f32[8,16,2,128]{3,2,1,0:T(2,128)S(1)}, f32[8,16,2,128]{3,2,1,0:T(2,128)S(1)}, u32[]{:S(2)}, u32[]{:S(2)}) %collective-permute-start) | collective-permute-done | bytes 131104 | tf_op jit(solution)/shard_map/ppermute | solution.py:27
  118.5 8.3 %collective-permute-done.1 = f32[8,16,2,128]{3,2,1,0:T(2,128)S(1)} collective-permute-done((f32[8,16,2,128]{3,2,1,0:T(2,128)S(1)}, f32[8,16,2,128]{3,2,1,0:T(2,128)S(1)}, u32[]{:S(2)}, u32[]{:S(2)}) %collective-permute-start.1) | collective-permute-done | bytes 131104 | tf_op jit(solution)/shard_map/ppermute | solution.py:27
  126.8 1.1 fusion.26
  128.1 1.1 fusion.27
  129.5 0.2 fusion.181
  129.7 0.4 multiply_add_fusion.7
  130.2 0.3 fusion.1
  130.5 0.3 multiply_add_fusion
  131.0 0.8 pad_maximum_fusion.33
  131.9 0.6 fusion.193
  136.1 0.2 fusion.189
  136.4 5.6 %collective-permute-start.7 = (f32[8,16,8,2]{3,2,1,0:T(8,128)S(1)}, f32[8,16,8,2]{3,2,1,0:T(8,128)S(1)}, u32[]{:S(2)}, u32[]{:S(2)}) collective-permute-start(f32[8,16,8,2]{3,2,1,0:T(8,128)S(1)} %get-tuple-element.244), channel_id=1, source_target_pairs={{8,0},{16,8},{24,16},{32,24},{40,32},{48,40},{56,48},{64,56},{72,6... | collective-permute-start | bytes 24584 | tf_op jit(solution)/shard_map/ppermute | solution.py:19
  142.0 0.3 fusion.104
  142.4 0.3 fusion.105
  143.3 6.6 %collective-permute-done.6 = f32[8,16,8,2]{3,2,1,0:T(8,128)S(1)} collective-permute-done((f32[8,16,8,2]{3,2,1,0:T(8,128)S(1)}, f32[8,16,8,2]{3,2,1,0:T(8,128)S(1)}, u32[]{:S(2)}, u32[]{:S(2)}) %collective-permute-start.6) | collective-permute-done | bytes 8224 | tf_op jit(solution)/shard_map/ppermute | solution.py:18
  149.8 3.6 %collective-permute-done.7 = f32[8,16,8,2]{3,2,1,0:T(8,128)S(1)} collective-permute-done((f32[8,16,8,2]{3,2,1,0:T(8,128)S(1)}, f32[8,16,8,2]{3,2,1,0:T(8,128)S(1)}, u32[]{:S(2)}, u32[]{:S(2)}) %collective-permute-start.7) | collective-permute-done | bytes 8224 | tf_op jit(solution)/shard_map/ppermute | solution.py:19
  153.4 1.1 fusion.160
  154.7 1.1 fusion.161
  155.8 0.3 multiply_reduce_fusion.2
  156.1 1.0 fusion.180
  157.1 0.9 fusion.179
  158.0 1.5 multiply_add_fusion.1
  159.5 62.7 %all-gather.5.cloned.1.call-done = f32[2,8,16,2,4096]{4,3,2,1,0:T(2,128)} async-done(((f32[2,8,16,2,128]{4,3,2,1,0:T(2,128)}), f32[2,8,16,2,4096]{4,3,2,1,0:T(2,128)}) %all-gather.5.cloned.1.call-update) | async-done | bytes 8388624 | tf_op jit(solution)/shard_map/all_gather | solution.py:118
  222.2 4.9 %constant_dynamic-update-slice_fusion.3 = f32[2,8,16,2,8192]{4,3,2,1,0:T(2,128)S(1)} fusion(f32[2,8,16,2,4096]{4,3,2,1,0:T(2,128)} %all-gather.5.cloned.1.call-done), kind=kLoop, calls=%fused_computation.408 | loop fusion | bytes 16777216
  227.1 1.0 copy-done.1
  228.1 1.2 constant_dynamic-update-slice_fusion.2
  229.5 1.8 fusion.175
  231.3 0.4 fusion.61
  231.7 1.8 collective-permute-start.4
  233.5 0.5 collective-permute-start.5
  234.1 0.4 fusion.10
  234.6 4.9 %collective-permute-done.4 = f32[8,16,2,128]{3,2,1,0:T(2,128)S(1)} collective-permute-done((f32[8,16,2,128]{3,2,1,0:T(2,128)S(1)}, f32[8,16,2,128]{3,2,1,0:T(2,128)S(1)}, u32[]{:S(2)}, u32[]{:S(2)}) %collective-permute-start.4) | collective-permute-done | bytes 131104 | tf_op jit(solution)/shard_map/ppermute | solution.py:27
  239.5 8.2 %collective-permute-done.5 = f32[8,16,2,128]{3,2,1,0:T(2,128)S(1)} collective-permute-done((f32[8,16,2,128]{3,2,1,0:T(2,128)S(1)}, f32[8,16,2,128]{3,2,1,0:T(2,128)S(1)}, u32[]{:S(2)}, u32[]{:S(2)}) %collective-permute-start.5) | collective-permute-done | bytes 131104 | tf_op jit(solution)/shard_map/ppermute | solution.py:27
  247.7 1.1 fusion.28
  248.9 1.1 fusion.29
  250.3 0.2 fusion.177
  250.6 0.4 multiply_add_fusion.3
  251.0 0.3 fusion.7
  251.3 1.1 fusion.21
  (98 shorter events, 2.8 us)
Async XLA Ops:
  6.5 93.9 %all-gather.3.cloned.1.call-start = ((), (), s32[]{:S(2)}) async-start(), calls=%async_computation | async-start | bytes 8650752 | tf_op jit(solution)/shard_map/all_gather | solution.py:118
  10.3 211.9 %all-gather.5.cloned.1.call-start = ((), (), s32[]{:S(2)}) async-start(), calls=%async_computation.1 | async-start | bytes 8650752 | tf_op jit(solution)/shard_map/all_gather | solution.py:118
  11.4 15.6 %collective-permute-start.2 = (f32[8,16,8,2]{3,2,1,0:T(8,128)}, f32[8,16,8,2]{3,2,1,0:T(8,128)S(1)}, u32[]{:S(2)}, u32[]{:S(2)}) collective-permute-start(f32[8,16,8,2]{3,2,1,0:T(8,128)} %get-tuple-element.255), channel_id=1, source_target_pairs={{0,8},{8,16},{16,24},{24,32},{32,40},{40,48},{48,56},{56,64},{64,7... | collective-permute-start | bytes 24584 | tf_op jit(solution)/shard_map/ppermute | solution.py:18
  11.4 15.6 %collective-permute-start.3 = (f32[8,16,8,2]{3,2,1,0:T(8,128)S(1)}, f32[8,16,8,2]{3,2,1,0:T(8,128)S(1)}, u32[]{:S(2)}, u32[]{:S(2)}) collective-permute-start(f32[8,16,8,2]{3,2,1,0:T(8,128)S(1)} %get-tuple-element.256), channel_id=1, source_target_pairs={{8,0},{16,8},{24,16},{32,24},{40,32},{48,40},{56,48},{64,56},{72,6... | collective-permute-start | bytes 24584 | tf_op jit(solution)/shard_map/ppermute | solution.py:19
  100.4 5.9 %copy-start = (f32[2,8,16,2,4096]{4,3,2,1,0:T(2,128)S(1)}, f32[2,8,16,2,4096]{4,3,2,1,0:T(2,128)}, u32[]{:S(2)}) copy-start(f32[2,8,16,2,4096]{4,3,2,1,0:T(2,128)} %all-gather.3.cloned.1.call-done) | copy-start | bytes 25165828
  107.6 7.1 %copy-start.8 = (f32[3,16,8,129]{3,2,1,0:T(8,128)S(1)}, f32[3,16,8,129]{3,2,1,0:T(8,128)}, u32[]{:S(2)}) copy-start(f32[3,16,8,129]{3,2,1,0:T(8,128)} %get-tuple-element.271) | copy-start | bytes 594436
  107.6 7.1 %copy-start.9 = (f32[3,16,8,129]{3,2,1,0:T(8,128)S(1)}, f32[3,16,8,129]{3,2,1,0:T(8,128)}, u32[]{:S(2)}) copy-start(f32[3,16,8,129]{3,2,1,0:T(8,128)} %get-tuple-element.272) | copy-start | bytes 594436
  107.6 7.1 %copy-start.10 = (f32[3,16,8,129]{3,2,1,0:T(8,128)S(1)}, f32[3,16,8,129]{3,2,1,0:T(8,128)}, u32[]{:S(2)}) copy-start(f32[3,16,8,129]{3,2,1,0:T(8,128)} %get-tuple-element.273) | copy-start | bytes 594436
  107.6 7.1 %copy-start.11 = (f32[3,16,8,129]{3,2,1,0:T(8,128)S(1)}, f32[3,16,8,129]{3,2,1,0:T(8,128)}, u32[]{:S(2)}) copy-start(f32[3,16,8,129]{3,2,1,0:T(8,128)} %get-tuple-element.274) | copy-start | bytes 594436
  107.6 7.1 %copy-start.16 = (f32[16,8,129]{2,1,0:T(8,128)S(1)}, f32[16,8,129]{2,1,0:T(8,128)}, u32[]{:S(2)}) copy-start(f32[16,8,129]{2,1,0:T(8,128)} %get-tuple-element.176) | copy-start | bytes 198148
  107.6 7.1 %copy-start.17 = (f32[1,16,8,129]{3,2,1,0:T(8,128)S(1)}, f32[1,16,8,129]{3,2,1,0:T(8,128)}, u32[]{:S(2)}) copy-start(f32[1,16,8,129]{3,2,1,0:T(8,128)} %get-tuple-element.177) | copy-start | bytes 198148
  107.6 7.1 %copy-start.18 = (f32[1,16,8,129]{3,2,1,0:T(8,128)S(1)}, f32[1,16,8,129]{3,2,1,0:T(8,128)}, u32[]{:S(2)}) copy-start(f32[1,16,8,129]{3,2,1,0:T(8,128)} %get-tuple-element.178) | copy-start | bytes 198148
  107.7 7.1 %copy-start.23 = (f32[1,16,8,129]{3,2,1,0:T(8,128)S(1)}, f32[1,16,8,129]{3,2,1,0:T(8,128)}, u32[]{:S(2)}) copy-start(f32[1,16,8,129]{3,2,1,0:T(8,128)} %get-tuple-element.182) | copy-start | bytes 198148
  107.7 7.1 %copy-start.24 = (f32[1,16,8,129]{3,2,1,0:T(8,128)S(1)}, f32[1,16,8,129]{3,2,1,0:T(8,128)}, u32[]{:S(2)}) copy-start(f32[1,16,8,129]{3,2,1,0:T(8,128)} %get-tuple-element.185) | copy-start | bytes 198148
  107.7 7.1 %copy-start.25 = (f32[1,16,8,129]{3,2,1,0:T(8,128)S(1)}, f32[1,16,8,129]{3,2,1,0:T(8,128)}, u32[]{:S(2)}) copy-start(f32[1,16,8,129]{3,2,1,0:T(8,128)} %get-tuple-element.186) | copy-start | bytes 198148
  107.7 7.1 %copy-start.26 = (f32[1,16,8,129]{3,2,1,0:T(8,128)S(1)}, f32[1,16,8,129]{3,2,1,0:T(8,128)}, u32[]{:S(2)}) copy-start(f32[1,16,8,129]{3,2,1,0:T(8,128)} %get-tuple-element.189) | copy-start | bytes 198148
  109.9 8.5 %collective-permute-start = (f32[8,16,2,128]{3,2,1,0:T(2,128)S(1)}, f32[8,16,2,128]{3,2,1,0:T(2,128)S(1)}, u32[]{:S(2)}, u32[]{:S(2)}) collective-permute-start(f32[8,16,2,128]{3,2,1,0:T(2,128)S(1)} %get-tuple-element.239), channel_id=1, source_target_pairs={{0,1},{1,2},{2,3},{3,4},{4,5},{5,6},{6,7},{7,0},{8,9},{9,10},{10,1... | collective-permute-start | bytes 393224 | tf_op jit(solution)/shard_map/ppermute | solution.py:27
  114.7 12.1 %collective-permute-start.1 = (f32[8,16,2,128]{3,2,1,0:T(2,128)S(1)}, f32[8,16,2,128]{3,2,1,0:T(2,128)S(1)}, u32[]{:S(2)}, u32[]{:S(2)}) collective-permute-start(f32[8,16,2,128]{3,2,1,0:T(2,128)S(1)} %get-tuple-element.240), channel_id=1, source_target_pairs={{0,7},{1,0},{2,1},{3,2},{4,3},{5,4},{6,5},{7,6},{8,15},{9,8},{10,9... | collective-permute-start | bytes 393224 | tf_op jit(solution)/shard_map/ppermute | solution.py:27
  129.2 1.3 copy-start.2
  136.3 13.6 %collective-permute-start.6 = (f32[8,16,8,2]{3,2,1,0:T(8,128)S(1)}, f32[8,16,8,2]{3,2,1,0:T(8,128)S(1)}, u32[]{:S(2)}, u32[]{:S(2)}) collective-permute-start(f32[8,16,8,2]{3,2,1,0:T(8,128)S(1)} %get-tuple-element.243), channel_id=1, source_target_pairs={{0,8},{8,16},{16,24},{24,32},{32,40},{40,48},{48,56},{56,64},{64,7... | collective-permute-start | bytes 24584 | tf_op jit(solution)/shard_map/ppermute | solution.py:18
  136.4 17.1 %collective-permute-start.7 = (f32[8,16,8,2]{3,2,1,0:T(8,128)S(1)}, f32[8,16,8,2]{3,2,1,0:T(8,128)S(1)}, u32[]{:S(2)}, u32[]{:S(2)}) collective-permute-start(f32[8,16,8,2]{3,2,1,0:T(8,128)S(1)} %get-tuple-element.244), channel_id=1, source_target_pairs={{8,0},{16,8},{24,16},{32,24},{40,32},{48,40},{56,48},{64,56},{72,6... | collective-permute-start | bytes 24584 | tf_op jit(solution)/shard_map/ppermute | solution.py:19
  222.2 5.9 %copy-start.1 = (f32[2,8,16,2,4096]{4,3,2,1,0:T(2,128)S(1)}, f32[2,8,16,2,4096]{4,3,2,1,0:T(2,128)}, u32[]{:S(2)}) copy-start(f32[2,8,16,2,4096]{4,3,2,1,0:T(2,128)} %all-gather.5.cloned.1.call-done) | copy-start | bytes 25165828
  229.3 4.7 %copy-start.3 = (f32[3,16,8,129]{3,2,1,0:T(8,128)S(1)}, f32[3,16,8,129]{3,2,1,0:T(8,128)}, u32[]{:S(2)}) copy-start(f32[3,16,8,129]{3,2,1,0:T(8,128)} %get-tuple-element.154) | copy-start | bytes 594436
  229.4 4.7 %copy-start.4 = (f32[3,16,8,129]{3,2,1,0:T(8,128)S(1)}, f32[3,16,8,129]{3,2,1,0:T(8,128)}, u32[]{:S(2)}) copy-start(f32[3,16,8,129]{3,2,1,0:T(8,128)} %get-tuple-element.279) | copy-start | bytes 594436
  229.4 4.7 %copy-start.5 = (f32[3,16,8,129]{3,2,1,0:T(8,128)S(1)}, f32[3,16,8,129]{3,2,1,0:T(8,128)}, u32[]{:S(2)}) copy-start(f32[3,16,8,129]{3,2,1,0:T(8,128)} %get-tuple-element.280) | copy-start | bytes 594436
  229.4 4.7 %copy-start.6 = (f32[3,16,8,129]{3,2,1,0:T(8,128)S(1)}, f32[3,16,8,129]{3,2,1,0:T(8,128)}, u32[]{:S(2)}) copy-start(f32[3,16,8,129]{3,2,1,0:T(8,128)} %get-tuple-element.281) | copy-start | bytes 594436
  229.4 4.7 %copy-start.7 = (f32[3,16,8,129]{3,2,1,0:T(8,128)S(1)}, f32[3,16,8,129]{3,2,1,0:T(8,128)}, u32[]{:S(2)}) copy-start(f32[3,16,8,129]{3,2,1,0:T(8,128)} %get-tuple-element.282) | copy-start | bytes 594436
  229.4 4.7 %copy-start.12 = (f32[1,16,8,129]{3,2,1,0:T(8,128)S(1)}, f32[1,16,8,129]{3,2,1,0:T(8,128)}, u32[]{:S(2)}) copy-start(f32[1,16,8,129]{3,2,1,0:T(8,128)} %get-tuple-element.137) | copy-start | bytes 198148
  229.4 4.7 %copy-start.13 = (f32[16,8,129]{2,1,0:T(8,128)S(1)}, f32[16,8,129]{2,1,0:T(8,128)}, u32[]{:S(2)}) copy-start(f32[16,8,129]{2,1,0:T(8,128)} %get-tuple-element.140) | copy-start | bytes 198148
  229.4 4.7 %copy-start.14 = (f32[1,16,8,129]{3,2,1,0:T(8,128)S(1)}, f32[1,16,8,129]{3,2,1,0:T(8,128)}, u32[]{:S(2)}) copy-start(f32[1,16,8,129]{3,2,1,0:T(8,128)} %get-tuple-element.141) | copy-start | bytes 198148
  229.4 4.7 %copy-start.15 = (f32[1,16,8,129]{3,2,1,0:T(8,128)S(1)}, f32[1,16,8,129]{3,2,1,0:T(8,128)}, u32[]{:S(2)}) copy-start(f32[1,16,8,129]{3,2,1,0:T(8,128)} %get-tuple-element.142) | copy-start | bytes 198148
  229.4 4.7 %copy-start.19 = (f32[1,16,8,129]{3,2,1,0:T(8,128)S(1)}, f32[1,16,8,129]{3,2,1,0:T(8,128)}, u32[]{:S(2)}) copy-start(f32[1,16,8,129]{3,2,1,0:T(8,128)} %get-tuple-element.146) | copy-start | bytes 198148
  229.4 4.7 %copy-start.20 = (f32[1,16,8,129]{3,2,1,0:T(8,128)S(1)}, f32[1,16,8,129]{3,2,1,0:T(8,128)}, u32[]{:S(2)}) copy-start(f32[1,16,8,129]{3,2,1,0:T(8,128)} %get-tuple-element.149) | copy-start | bytes 198148
  229.5 4.7 %copy-start.21 = (f32[1,16,8,129]{3,2,1,0:T(8,128)S(1)}, f32[1,16,8,129]{3,2,1,0:T(8,128)}, u32[]{:S(2)}) copy-start(f32[1,16,8,129]{3,2,1,0:T(8,128)} %get-tuple-element.150) | copy-start | bytes 198148
  229.5 4.7 %copy-start.22 = (f32[1,16,8,129]{3,2,1,0:T(8,128)S(1)}, f32[1,16,8,129]{3,2,1,0:T(8,128)}, u32[]{:S(2)}) copy-start(f32[1,16,8,129]{3,2,1,0:T(8,128)} %get-tuple-element.153) | copy-start | bytes 198148
  231.7 7.8 %collective-permute-start.4 = (f32[8,16,2,128]{3,2,1,0:T(2,128)S(1)}, f32[8,16,2,128]{3,2,1,0:T(2,128)S(1)}, u32[]{:S(2)}, u32[]{:S(2)}) collective-permute-start(f32[8,16,2,128]{3,2,1,0:T(2,128)S(1)} %get-tuple-element.237), channel_id=1, source_target_pairs={{0,1},{1,2},{2,3},{3,4},{4,5},{5,6},{6,7},{7,0},{8,9},{9,10},{10,1... | collective-permute-start | bytes 393224 | tf_op jit(solution)/shard_map/ppermute | solution.py:27
  233.5 14.2 %collective-permute-start.5 = (f32[8,16,2,128]{3,2,1,0:T(2,128)S(1)}, f32[8,16,2,128]{3,2,1,0:T(2,128)S(1)}, u32[]{:S(2)}, u32[]{:S(2)}) collective-permute-start(f32[8,16,2,128]{3,2,1,0:T(2,128)S(1)} %get-tuple-element.238), channel_id=1, source_target_pairs={{0,7},{1,0},{2,1},{3,2},{4,3},{5,4},{6,5},{7,6},{8,15},{9,8},{10,9... | collective-permute-start | bytes 393224 | tf_op jit(solution)/shard_map/ppermute | solution.py:27
Sparse Core Ops, SparseCore 0:
  10.5 89.9 all-gather.2
  132.0 90.1 all-gather.4
where the time goes:
time: 259 us
  waiting for transfers between devices  165 us (64%)
  other arithmetic  29.6 us (11%)
  local copies, waits for them, and re-layouts  22.7 us (9%)
  between operations  22.7 us (9%)
  starting transfers between devices  19.1 us (7%)
    all_gather x2, waiting for transfers between devices, section(): gathered = lax.all_gather(strips, 'az', axis=4, tiled=True)  130 us
    ppermute x4, waiting for transfers between devices, shifted_2(): return lax.ppermute(value, axis, pairs)  24.7 us
    unnamed x56, local copies, waits for them, and re-layouts  11.9 us
    ppermute x2, starting transfers between devices, padded_2(): after = lax.ppermute(first, axis, down)  11.9 us
    ppermute x4, starting transfers between devices, shifted_2(): return lax.ppermute(value, axis, pairs)  7.06 us
    ppermute x2, waiting for transfers between devices, padded_2(): before = lax.ppermute(last, axis, up)  6.57 us
  transfers between devices with their start and end apart: 10, of which 8 were waited for; matrix products, arithmetic and copies ran while one was open for 8% of the time, Pallas kernels for 0%

commit v1 on v0

v1 whole, which is shorter than its diff:
```python
import functools

import jax
import jax.numpy as jnp
from jax import lax
from jax.experimental import pallas as pl
from jax.experimental.pallas import tpu as pltpu
from jax.sharding import PartitionSpec as P

MESH = pl.DeviceIdType.MESH
time_step = 0.02
shear_jump = 0.5
AZ, RAD = 32, 8
NF, NX, NZ, NY = 8, 8, 16, 128
COLS = AZ * NY


def primitive_of(u):
    inv = 1.0 / u[0]
    v = [u[i] * inv for i in (1, 2, 3)]
    vv = v[0] * v[0] + v[1] * v[1] + v[2] * v[2]
    bb = u[5] * u[5] + u[6] * u[6] + u[7] * u[7]
    p = (2.0 / 3.0) * (u[4] - 0.5 * u[0] * vv - 0.5 * bb)
    return [u[0], v[0], v[1], v[2], p, u[5], u[6], u[7]]


def half_slope(a, b):
    return 0.5 * jnp.maximum(jnp.minimum(a, b), jnp.minimum(jnp.maximum(a, b), 0.0))


def state_of(w, n):
    rho, v, p, b = w[0], w[1:4], w[4], w[5:8]
    vn, bn = v[n], b[n]
    bb = b[0] * b[0] + b[1] * b[1] + b[2] * b[2]
    hb = 0.5 * bb
    vv = v[0] * v[0] + v[1] * v[1] + v[2] * v[2]
    vb = v[0] * b[0] + v[1] * b[1] + v[2] * b[2]
    pt = p + hb
    mom = [rho * c for c in v]
    en = 1.5 * p + 0.5 * rho * vv + hb
    fm = [mom[i] * vn - b[i] * bn for i in range(3)]
    fm[n] = fm[n] + pt
    fe = (en + pt) * vn - bn * vb
    fb = [None if i == n else b[i] * vn - v[i] * bn for i in range(3)]
    a = (5.0 / 3.0) * p + bb
    speed = jnp.abs(vn) + (a * lax.rsqrt(a)) * lax.rsqrt(rho)
    return [rho] + mom + [en] + list(b), [mom[n]] + fm + [fe] + fb, speed


def twice_flux(left, right, n):
    ul, fl, cl = state_of(left, n)
    ur, fr, cr = state_of(right, n)
    c = jnp.maximum(cl, cr)
    out = []
    for i in range(NF):
        diff = c * (ur[i] - ul[i])
        out.append(-diff if fl[i] is None else fl[i] + fr[i] - diff)
    return out


def rolled_faces(w, axis, n):
    size = w[0].shape[axis]
    left, right = [], []
    for f in range(NF):
        d = w[f] - pltpu.roll(w[f], 1, axis)
        h = half_slope(d, pltpu.roll(d, size - 1, axis))
        left.append(pltpu.roll(w[f] + h, 1, axis))
        right.append(w[f] - h)
    return twice_flux(left, right, n)


def kernel(shift_ref, u_hbm, out_ref, raw, w1, w2, acc, fx, tend, corr, strips, y_lo, y_hi, ghost, relay_in, relay_roll,
           relay_out, in_sem, x_send, x_recv, y_send, y_recv, a_send, a_recv, b_send):
    az = lax.axis_index("az")
    rad = lax.axis_index("rad")
    right, left = (az + 1) % AZ, (az + AZ - 1) % AZ
    edge = (rad == 0) | (rad == RAD - 1)
    relay_lo = rad == 4 + az % 3
    relay_hi = rad == 3 - az % 3
    relay = relay_lo | relay_hi
    kick = [jnp.where(rad == 0, shear_jump, 0.0), jnp.where(rad == RAD - 1, -shear_jump, 0.0)]

    load = pltpu.make_async_copy(u_hbm, raw, in_sem)
    load.start()

    barrier = pltpu.get_barrier_semaphore()

    def signal(*device):
        pl.semaphore_signal(barrier, 1, device_id=device, device_id_type=MESH)

    signal(right, rad)
    signal(left, rad)

    @pl.when(edge)
    def _():
        def step(k, carry):
            p = (k + az) % AZ
            signal(p, 4 + p % 3)
            signal(p, 3 - p % 3)
            return carry
        lax.fori_loop(0, AZ, step, 0)

    @pl.when(relay)
    def _():
        def step(k, carry):
            p = (k + az) % AZ
            signal(p, 0)
            signal(p, RAD - 1)
            return carry
        lax.fori_loop(0, AZ, step, 0)

    @pl.when(rad > 0)
    def _():
        signal(az, rad - 1)

    @pl.when(rad < RAD - 1)
    def _():
        signal(az, rad + 1)

    lane = lax.broadcasted_iota(jnp.int32, (NZ, NY), 1)
    slot = lane % 16
    block = lane // 16
    inner = (lane > 1) & (lane < NY - 1)
    seam = (lane < 2) | (lane >= NY - 2)

    load.wait()
    u_rows = raw.reshape(NF * NZ * NX, NY)

    def conserved_row(x):
        return [u_rows[pl.ds(f * NZ * NX + x, NZ, NX), :] for f in range(NF)]

    def first_rows(x, carry):
        w = primitive_of(conserved_row(x))
        for f in range(NF):
            w1[f, x + 2] = w[f]
        return carry

    lax.fori_loop(0, NX, first_rows, 0)

    pl.semaphore_wait(barrier, jnp.where(edge, 2 * AZ + 3, jnp.where(relay, 2 * AZ + 4, 4)))

    def x_copy(sec, w, up):
        rows = w.at[:, pl.ds(8 if up else 2, 2)]
        side = 0 if up else 1
        return pltpu.make_async_remote_copy(
            rows, ghost.at[sec, side], x_send.at[sec, side], x_recv.at[sec, side],
            device_id=(az, rad + 1 if up else rad - 1), device_id_type=MESH)

    def y_copy(sec, up):
        return pltpu.make_async_remote_copy(
            strips.at[sec], (y_lo if up else y_hi).at[sec], y_send.at[sec, 0 if up else 1],
            y_recv.at[sec, 0 if up else 1],
            device_id=(right if up else left, rad), device_id_type=MESH)

    def start_x(sec, w):
        @pl.when(edge)
        def _():
            base = jnp.where(rad == 0, 2, 8)

            def step(k, carry):
                p = (k + az) % AZ
                f, j, half = p // 4, (p // 2) % 2, p % 2
                pltpu.make_async_remote_copy(
                    w.at[f, base + j, pl.ds(pl.multiple_of(half * 8, 8), 8)], relay_in.at[sec, az],
                    a_send.at[sec], a_recv.at[sec],
                    device_id=(p, jnp.where(rad == 0, 3 - p % 3, 4 + p % 3)), device_id_type=MESH).start()
                return carry

            lax.fori_loop(0, AZ, step, 0)

        @pl.when(rad < RAD - 1)
        def _():
            x_copy(sec, w, True).start()

        @pl.when(rad > 0)
        def _():
            x_copy(sec, w, False).start()

    def start_y(sec, w):
        for f in range(NF):
            q = w[f, 2]
            q = pltpu.roll(q, 8, 1)
            for x in range(1, NX):
                q = jnp.where(block == x, pltpu.roll(w[f, x + 2], (16 * x + 8) % NY, 1), q)
            strips[sec, f] = q
        y_copy(sec, True).start()
        y_copy(sec, False).start()

    def serve(sec):
        @pl.when(relay)
        def _():
            offset = shift_ref[sec]
            amount = jnp.where(relay_lo, offset, (COLS - offset) % COLS)
            whole, part = amount // NY, amount % NY
            pltpu.make_async_copy(relay_in.at[sec], relay_in.at[sec], a_recv.at[sec]).wait()

            def turn(k, carry):
                relay_roll[k] = pltpu.roll(relay_in[sec, k], (NY - part) % NY, 1)
                return carry

            lax.fori_loop(0, AZ, turn, 0, unroll=4)
            keep = lax.broadcasted_iota(jnp.int32, (8, NY), 1) < NY - part
            f, j, half = az // 4, (az // 2) % 2, az % 2
            side = jnp.where(relay_lo, 0, 1)
            target = jnp.where(relay_lo, 0, RAD - 1)

            def step(k, carry):
                d = (k + az) % AZ
                relay_out[sec, d] = jnp.where(
                    keep, relay_roll[(d + whole) % AZ], relay_roll[(d + whole + 1) % AZ])
                pltpu.make_async_remote_copy(
                    relay_out.at[sec, d],
                    ghost.at[sec, side, f, j, pl.ds(pl.multiple_of(half * 8, 8), 8)],
                    b_send.at[sec], x_recv.at[sec, side],
                    device_id=(d, target), device_id_type=MESH).start()
                return carry

            lax.fori_loop(0, AZ, step, 0)

    def inside(w):
        def row(x, carry):
            cells = [w[f, x + 2] for f in range(NF)]
            flux = rolled_faces(cells, 0, 2)
            for f in range(NF):
                acc[f, x] = pltpu.roll(flux[f], NZ - 1, 0) - flux[f]
            flux = rolled_faces(cells, 1, 1)
            for f in range(NF):
                masked = jnp.where(inner, flux[f], 0.0)
                acc[f, x] += pltpu.roll(masked, NY - 1, 1) - masked
            return carry

        lax.fori_loop(0, NX, row, 0)

    def x_faces(w, begin, end):
        def face(i, carry):
            lefts, rights = [], []
            for f in range(NF):
                c = [w[f, i + k] for k in range(4)]
                d = [c[k + 1] - c[k] for k in range(3)]
                lefts.append(c[1] + half_slope(d[0], d[1]))
                rights.append(c[2] - half_slope(d[1], d[2]))
            flux = twice_flux(lefts, rights, 0)
            for f in range(NF):
                fx[f, i] = flux[f]
            return carry

        lax.fori_loop(begin, end, face, 0)

    def finish_y(sec):
        y_copy(sec, True).wait_recv()
        y_copy(sec, False).wait_recv()
        cells = []
        for f in range(NF):
            own = strips[sec, f]
            lower = jnp.where((slot >= 4) & (slot < 8), y_lo[sec, f], own)
            upper = jnp.where((slot >= 8) & (slot < 12), y_hi[sec, f], own)
            cells.append(jnp.where(slot < 8, pltpu.roll(lower, NY - 4, 1), pltpu.roll(upper, 4, 1)))
        flux = rolled_faces(cells, 1, 1)
        for f in range(NF):
            masked = jnp.where((slot == 4) | (slot == 5) | (slot == 11) | (slot == 12), flux[f], 0.0)
            d = pltpu.roll(masked, NY - 1, 1) - masked
            far = pltpu.roll(d, NY - 8, 1)
            corr[f] = jnp.where((slot == 4) | (slot == 5), d, jnp.where((slot == 2) | (slot == 3), far, 0.0))
        for f in range(NF):
            value = corr[f]
            for x in range(NX):
                acc[f, x] += jnp.where(seam, pltpu.roll(value, (124 - 16 * x) % NY, 1), 0.0)

    def receive_x(sec, w):
        for side in range(2):
            pltpu.make_async_copy(ghost.at[sec, side], ghost.at[sec, side], x_recv.at[sec, side]).wait()
            for f in range(NF):
                for j in range(2):
                    value = ghost[sec, side, f, j]
                    if f == 2:
                        value = value + kick[side]
                    w[f, j + (10 if side else 0)] = value

    def row_total(x):
        return [-0.5 * (acc[f, x] + (fx[f, x + 1] - fx[f, x])) for f in range(NF)]

    def middle(x, carry):
        total = row_total(x)
        u = conserved_row(x)
        w = primitive_of([u[f] + time_step * total[f] for f in range(NF)])
        for f in range(NF):
            tend[f, x] = total[f]
            w2[f, x + 2] = w[f]
        return carry

    out_rows = out_ref.reshape(NF * NZ * NX, NY)

    def last(x, carry):
        total = row_total(x)
        for f in range(NF):
            out_rows[pl.ds(f * NZ * NX + x, NZ, NX), :] = 0.5 * (tend[f, x] + total[f])
        return carry

    for sec, w, end in ((0, w1, middle), (1, w2, last)):
        start_x(sec, w)
        start_y(sec, w)
        inside(w)
        x_faces(w, 2, 7)
        serve(sec)
        finish_y(sec)
        lax.fori_loop(2, 6, end, 0)
        receive_x(sec, w)
        x_faces(w, 0, 2)
        x_faces(w, 7, 9)
        lax.fori_loop(0, 2, end, 0)
        lax.fori_loop(6, 8, end, 0)

    for sec, w in ((0, w1), (1, w2)):
        y_copy(sec, True).wait_send()
        y_copy(sec, False).wait_send()

        @pl.when(rad < RAD - 1)
        def _():
            x_copy(sec, w, True).wait_send()

        @pl.when(rad > 0)
        def _():
            x_copy(sec, w, False).wait_send()

        @pl.when(edge)
        def _():
            pltpu.make_async_copy(relay_in.at[sec], relay_in.at[sec], a_send.at[sec]).wait()

        @pl.when(relay)
        def _():
            pltpu.make_async_copy(relay_out.at[sec], relay_out.at[sec], b_send.at[sec]).wait()


def shards(conserved, shear_shift):
    f32 = jnp.float32
    return pl.pallas_call(
        kernel,
        out_shape=jax.ShapeDtypeStruct((NF, NZ, NX, NY), f32),
        in_specs=[pl.BlockSpec(memory_space=pltpu.SMEM), pl.BlockSpec(memory_space=pl.ANY)],
        out_specs=pl.BlockSpec(memory_space=pltpu.VMEM),
        scratch_shapes=[
            pltpu.VMEM((NF, NZ, NX, NY), f32),
            pltpu.VMEM((NF, NX + 4, NZ, NY), f32),
            pltpu.VMEM((NF, NX + 4, NZ, NY), f32),
            pltpu.VMEM((NF, NX, NZ, NY), f32),
            pltpu.VMEM((NF, NX + 1, NZ, NY), f32),
            pltpu.VMEM((NF, NX, NZ, NY), f32),
            pltpu.VMEM((NF, NZ, NY), f32),
            pltpu.VMEM((2, NF, NZ, NY), f32),
            pltpu.VMEM((2, NF, NZ, NY), f32),
            pltpu.VMEM((2, NF, NZ, NY), f32),
            pltpu.VMEM((2, 2, NF, 2, NZ, NY), f32),
            pltpu.VMEM((2, AZ, 8, NY), f32),
            pltpu.VMEM((AZ, 8, NY), f32),
            pltpu.VMEM((2, AZ, 8, NY), f32),
            pltpu.SemaphoreType.DMA,
            pltpu.SemaphoreType.DMA((2, 2)),
            pltpu.SemaphoreType.DMA((2, 2)),
            pltpu.SemaphoreType.DMA((2, 2)),
            pltpu.SemaphoreType.DMA((2, 2)),
            pltpu.SemaphoreType.DMA((2,)),
            pltpu.SemaphoreType.DMA((2,)),
            pltpu.SemaphoreType.DMA((2,)),
        ],
        name="mhd_step",
        compiler_params=pltpu.CompilerParams(
            collective_id=0, has_side_effects=True, vmem_limit_bytes=32 * 1024 * 1024),
    )(shear_shift, conserved)


def solution(mesh):
    return jax.shard_map(
        shards,
        mesh=mesh,
        in_specs=(P(None, None, "rad", "az"), P()),
        out_specs=P(None, None, "rad", "az"),
        check_vma=False,
    )
```

time: 259 us -> 50.5 us (0.19)
  the two profiles are of different devices: /device:TPU:24 before, /device:TPU:1 now
where the time goes in v1:
time: 50.5 us; the launch traced here: 50.4 us
  Pallas kernels  47.9 us (95%)
  local copies, waits for them, and re-layouts  2.49 us (5%)
    pallas_call x1, Pallas kernels, shards(): pl.pallas_call(kernel, out_shape=jax.ShapeDtypeStruct((NF, NZ, NX, NY), f...  47.9 us
    unnamed x5, local copies, waits for them, and re-layouts  2.49 us

profile of v1, /device:TPU:1, one launch (start us, length us, event | category | flops | bytes accessed | tf_op | source)
XLA Modules:
  0.0 50.4 jit_solution(13091973723943299304)
XLA Ops:
  0.0 0.0 copy-start
  0.0 1.0 %copy-done = f32[8,16,8,128]{3,2,1,0:T(8,128)S(1)} copy-done((f32[8,16,8,128]{3,2,1,0:T(8,128)S(1)}, f32[8,16,8,128]{3,2,1,0:T(8,128)}, u32[]{:S(2)}) %copy-start) | copy-done | bytes 524312
  1.0 0.0 copy-start.1
  1.0 0.7 %copy-done.1 = s32[2]{0:T(128)S(1)} copy-done((s32[2]{0:T(128)S(1)}, s32[2]{0:T(128)}, u32[]{:S(2)}) %copy-start.1) | copy-done | bytes 32
  1.7 47.9 %mhd_step.1 = f32[8,16,8,128]{3,2,1,0:T(8,128)S(1)} custom-call(s32[2]{0:T(128)S(1)} %copy-done.1, f32[8,16,8,128]{3,2,1,0:T(8,128)S(1)} %copy-done), custom_call_target="tpu_custom_call" | custom-call | tf_op jit(solution)/shard_map/mhd_step/pallas_call | solution.py:336
  49.6 0.8 %copy.4 = f32[8,16,8,128]{3,2,1,0:T(8,128)} copy(f32[8,16,8,128]{3,2,1,0:T(8,128)S(1)} %mhd_step.1) | data formatting | bytes 1048576
Async XLA Ops:
  0.0 1.0 %copy-start = (f32[8,16,8,128]{3,2,1,0:T(8,128)S(1)}, f32[8,16,8,128]{3,2,1,0:T(8,128)}, u32[]{:S(2)}) copy-start(f32[8,16,8,128]{3,2,1,0:T(8,128)} %u_hbm.1) | copy-start | bytes 1572868
  1.0 0.7 %copy-start.1 = (s32[2]{0:T(128)S(1)}, s32[2]{0:T(128)}, u32[]{:S(2)}) copy-start(s32[2]{0:T(128)} %shift_ref.1) | copy-start | bytes 28

commit v2 on v1

--- a/solution.py
+++ b/solution.py
@@ -22,6 +22,13 @@
     bb = u[5] * u[5] + u[6] * u[6] + u[7] * u[7]
     p = (2.0 / 3.0) * (u[4] - 0.5 * u[0] * vv - 0.5 * bb)
     return [u[0], v[0], v[1], v[2], p, u[5], u[6], u[7]]
+
+
+def conserved_of(w):
+    rho, v, p, b = w[0], w[1:4], w[4], w[5:8]
+    vv = v[0] * v[0] + v[1] * v[1] + v[2] * v[2]
+    bb = b[0] * b[0] + b[1] * b[1] + b[2] * b[2]
+    return [rho] + [rho * c for c in v] + [1.5 * p + 0.5 * rho * vv + 0.5 * bb] + list(b)
 
 
 def half_slope(a, b):
@@ -69,8 +76,31 @@
     return twice_flux(left, right, n)
 
 
-def kernel(shift_ref, u_hbm, out_ref, raw, w1, w2, acc, fx, tend, corr, strips, y_lo, y_hi, ghost, relay_in, relay_roll,
-           relay_out, in_sem, x_send, x_recv, y_send, y_recv, a_send, a_recv, b_send):
+def ghosted_divergence(w, g, lane, n):
+    size = w[0].shape[1]
+    first, final = lane == 0, lane == size - 1
+    left, right, left_g, right_g = [], [], [], []
+    for f in range(NF):
+        w_up, g_up = pltpu.roll(w[f], 1, 1), pltpu.roll(g[f], 1, 1)
+        d = w[f] - jnp.where(first, g_up, w_up)
+        d_g = g[f] - jnp.where(first, w_up, g_up)
+        d_down, d_g_down = pltpu.roll(d, size - 1, 1), pltpu.roll(d_g, size - 1, 1)
+        h = half_slope(d, jnp.where(final, d_g_down, d_down))
+        h_g = half_slope(d_g, jnp.where(final, d_down, d_g_down))
+        l_up = pltpu.roll(w[f] + h, 1, 1)
+        left.append(jnp.where(first, pltpu.roll(g[f] + h_g, 1, 1), l_up))
+        right.append(w[f] - h)
+        left_g.append(l_up)
+        right_g.append(g[f] - h_g)
+    flux = twice_flux(left, right, n)
+    flux_g = twice_flux(left_g, right_g, n)
+    return [jnp.where(final, pltpu.roll(flux_g[f], size - 1, 1), pltpu.roll(flux[f], size - 1, 1)) - flux[f]
+            for f in range(NF)]
+
+
+def kernel(shift_hbm, u_hbm, out_ref, raw, w1, w2, acc, fx, tend, corr, strips, y_lo, y_hi, ghost, stage, relay_in,
+           relay_roll, near_out, far_out, plane_out, far_in, plane_in, ext_rows, ext_flux, shift_ref, in_sem, shift_sem,
+           x_send, x_recv, y_send, y_recv, a_send, a_recv, b_send, far_send, far_recv, plane_send, plane_recv):
     az = lax.axis_index("az")
     rad = lax.axis_index("rad")
     right, left = (az + 1) % AZ, (az + AZ - 1) % AZ
@@ -80,16 +110,35 @@
     relay = relay_lo | relay_hi
     kick = [jnp.where(rad == 0, shear_jump, 0.0), jnp.where(rad == RAD - 1, -shear_jump, 0.0)]
 
+    barrier = pltpu.get_barrier_semaphore()
+
+    def signal(*device):
+        pl.semaphore_signal(barrier, 1, device_id=device, device_id_type=MESH)
+
     load = pltpu.make_async_copy(u_hbm, raw, in_sem)
     load.start()
-
-    barrier = pltpu.get_barrier_semaphore()
-
-    def signal(*device):
-        pl.semaphore_signal(barrier, 1, device_id=device, device_id_type=MESH)
+    load_shift = pltpu.make_async_copy(shift_hbm, shift_ref, shift_sem)
+    load_shift.start()
+
+    @pl.when(relay)
+    def _():
+        source = jnp.where(relay_lo, RAD - 1, 0)
+
+        def step(k, carry):
+            signal((k + az) % AZ, source)
+            return carry
+        lax.fori_loop(0, AZ, step, 0)
 
     signal(right, rad)
     signal(left, rad)
+
+    @pl.when(rad > 0)
+    def _():
+        signal(az, rad - 1)
+
+    @pl.when(rad < RAD - 1)
+    def _():
+        signal(az, rad + 1)
 
     @pl.when(edge)
     def _():
@@ -100,23 +149,6 @@
             return carry
         lax.fori_loop(0, AZ, step, 0)
 
-    @pl.when(relay)
-    def _():
-        def step(k, carry):
-            p = (k + az) % AZ
-            signal(p, 0)
-            signal(p, RAD - 1)
-            return carry
-        lax.fori_loop(0, AZ, step, 0)
-
-    @pl.when(rad > 0)
-    def _():
-        signal(az, rad - 1)
-
-    @pl.when(rad < RAD - 1)
-    def _():
-        signal(az, rad + 1)
-
     lane = lax.broadcasted_iota(jnp.int32, (NZ, NY), 1)
     slot = lane % 16
     block = lane // 16
@@ -137,7 +169,17 @@
 
     lax.fori_loop(0, NX, first_rows, 0)
 
-    pl.semaphore_wait(barrier, jnp.where(edge, 2 * AZ + 3, jnp.where(relay, 2 * AZ + 4, 4)))
+    @pl.when(edge)
+    def _():
+        near, far = jnp.where(rad == 0, 2, 8), jnp.where(rad == 0, 4, 6)
+        for f in range(NF):
+            for j in range(2):
+                for t, base in ((0, near), (1, far)):
+                    row = w1[f, base + j]
+                    for half in range(2):
+                        stage[f * 4 + j * 2 + half, t] = row[half * 8:half * 8 + 8]
+
+    pl.semaphore_wait(barrier, jnp.where(edge, AZ + 3, jnp.where(relay, 2 * AZ + 4, 4)))
 
     def x_copy(sec, w, up):
         rows = w.at[:, pl.ds(8 if up else 2, 2)]
@@ -152,22 +194,19 @@
             y_recv.at[sec, 0 if up else 1],
             device_id=(right if up else left, rad), device_id_type=MESH)
 
-    def start_x(sec, w):
+    def scatter():
         @pl.when(edge)
         def _():
-            base = jnp.where(rad == 0, 2, 8)
-
             def step(k, carry):
                 p = (k + az) % AZ
-                f, j, half = p // 4, (p // 2) % 2, p % 2
                 pltpu.make_async_remote_copy(
-                    w.at[f, base + j, pl.ds(pl.multiple_of(half * 8, 8), 8)], relay_in.at[sec, az],
-                    a_send.at[sec], a_recv.at[sec],
+                    stage.at[p], relay_in.at[az], a_send, a_recv,
                     device_id=(p, jnp.where(rad == 0, 3 - p % 3, 4 + p % 3)), device_id_type=MESH).start()
                 return carry
 
             lax.fori_loop(0, AZ, step, 0)
 
+    def start_x(sec, w):
         @pl.when(rad < RAD - 1)
         def _():
             x_copy(sec, w, True).start()
@@ -186,36 +225,76 @@
         y_copy(sec, True).start()
         y_copy(sec, False).start()
 
-    def serve(sec):
+    def serve():
         @pl.when(relay)
         def _():
-            offset = shift_ref[sec]
-            amount = jnp.where(relay_lo, offset, (COLS - offset) % COLS)
-            whole, part = amount // NY, amount % NY
-            pltpu.make_async_copy(relay_in.at[sec], relay_in.at[sec], a_recv.at[sec]).wait()
-
-            def turn(k, carry):
-                relay_roll[k] = pltpu.roll(relay_in[sec, k], (NY - part) % NY, 1)
+            def signed(s):
+                return jnp.where(relay_lo, s, COLS - s) % COLS
+
+            shift_0, shift_1 = signed(shift_ref[0]), signed(shift_ref[1])
+            f, j, half = az // 4, (az // 2) % 2, az % 2
+            rows = pl.ds(pl.multiple_of(half * 8, 8), 8)
+            side = jnp.where(relay_lo, 0, 1)
+            across = jnp.where(relay_lo, 0, RAD - 1)
+            small = lax.broadcasted_iota(jnp.int32, (8, NY), 1)
+            pltpu.make_async_copy(relay_in, relay_in, a_recv).wait()
+
+            def turn(slots, tiles, amount):
+                part = amount % NY
+
+                def step(k, carry):
+                    for c, t in zip(slots, tiles):
+                        relay_roll[c, k] = pltpu.roll(relay_in[k, t], (NY - part) % NY, 1)
+                    return carry
+
+                lax.fori_loop(0, AZ, step, 0, unroll=4)
+
+            def pick(c, d, amount):
+                whole, part = amount // NY, amount % NY
+                return jnp.where(
+                    small < NY - part, relay_roll[c, (d + whole) % AZ], relay_roll[c, (d + whole + 1) % AZ])
+
+            turn((0,), (0,), shift_0)
+
+            def near_step(k, carry):
+                d = (k + az) % AZ
+                near_out[d] = pick(0, d, shift_0)
+                pltpu.make_async_remote_copy(
+                    near_out.at[d], ghost.at[0, side, f, j, rows], b_send, x_recv.at[0, side],
+                    device_id=(d, across), device_id_type=MESH).start()
                 return carry
 
-            lax.fori_loop(0, AZ, turn, 0, unroll=4)
-            keep = lax.broadcasted_iota(jnp.int32, (8, NY), 1) < NY - part
-            f, j, half = az // 4, (az // 2) % 2, az % 2
-            side = jnp.where(relay_lo, 0, 1)
-            target = jnp.where(relay_lo, 0, RAD - 1)
-
-            def step(k, carry):
+            lax.fori_loop(0, AZ, near_step, 0)
+            turn((0, 1), (0, 1), shift_1)
+
+            def pick_step(d, carry):
+                for t in range(2):
+                    far_out[d, t] = pick(t, d, shift_1)
+                return carry
+
+            lax.fori_loop(0, AZ, pick_step, 0)
+
+            def far_step(k, carry):
                 d = (k + az) % AZ
-                relay_out[sec, d] = jnp.where(
-                    keep, relay_roll[(d + whole) % AZ], relay_roll[(d + whole + 1) % AZ])
+                far_out[d, 2] = jnp.where(small < NY // 2, far_out[(d + 1) % AZ, 0], far_out[(d + AZ - 1) % AZ, 0])
                 pltpu.make_async_remote_copy(
-                    relay_out.at[sec, d],
-                    ghost.at[sec, side, f, j, pl.ds(pl.multiple_of(half * 8, 8), 8)],
-                    b_send.at[sec], x_recv.at[sec, side],
-                    device_id=(d, target), device_id_type=MESH).start()
+                    far_out.at[d], far_in.at[:, f, j, rows], far_send, far_recv,
+                    device_id=(d, across), device_id_type=MESH).start()
                 return carry
 
-            lax.fori_loop(0, AZ, step, 0)
+            lax.fori_loop(0, AZ, far_step, 0)
+            shift_2 = (shift_0 - shift_1 + COLS) % COLS
+            turn((0,), (0,), shift_2)
+
+            def plane_step(k, carry):
+                d = (k + az) % AZ
+                plane_out[d] = pick(0, d, shift_2)
+                pltpu.make_async_remote_copy(
+                    plane_out.at[d], plane_in.at[f, j, rows], plane_send, plane_recv,
+                    device_id=(d, RAD - 1 - across), device_id_type=MESH).start()
+                return carry
+
+            lax.fori_loop(0, AZ, plane_step, 0)
 
     def inside(w):
         def row(x, carry):
@@ -231,7 +310,7 @@
 
         lax.fori_loop(0, NX, row, 0)
 
-    def x_faces(w, begin, end):
+    def x_faces(w, flux_ref, begin, end):
         def face(i, carry):
             lefts, rights = [], []
             for f in range(NF):
@@ -241,7 +320,7 @@
                 rights.append(c[2] - half_slope(d[1], d[2]))
             flux = twice_flux(lefts, rights, 0)
             for f in range(NF):
-                fx[f, i] = flux[f]
+                flux_ref[f, i] = flux[f]
             return carry
 
         lax.fori_loop(begin, end, face, 0)
@@ -266,15 +345,64 @@
             for x in range(NX):
                 acc[f, x] += jnp.where(seam, pltpu.roll(value, (124 - 16 * x) % NY, 1), 0.0)
 
+    def receive_side(sec, w, side):
+        pltpu.make_async_copy(ghost.at[sec, side], ghost.at[sec, side], x_recv.at[sec, side]).wait()
+        for f in range(NF):
+            for j in range(2):
+                value = ghost[sec, side, f, j]
+                if f == 2:
+                    value = value + kick[side]
+                w[f, j + (10 if side else 0)] = value
+
+    def sheared_rows(w):
+        pltpu.make_async_copy(plane_in, plane_in, plane_recv).wait()
+        pltpu.make_async_copy(far_in, far_in, far_recv).wait()
+        far_at = jnp.where(rad == 0, 0, 4)
+        plane_kick = jnp.where(rad == 0, -shear_jump, shear_jump)
+        for f in range(NF):
+            for j in range(2):
+                ext_rows[f, 2 + j] = far_in[0, f, j]
+                ext_rows[f, far_at + j] = far_in[1, f, j]
+                value = plane_in[f, j]
+                if f == 2:
+                    value = value + plane_kick
+                ext_rows[f, 4 - far_at + j] = value
+        x_faces(ext_rows, ext_flux, 0, 3)
+
+        def row(j, carry):
+            cells = [ext_rows[f, 2 + j] for f in range(NF)]
+            flux = rolled_faces(cells, 0, 2)
+            part = ghosted_divergence(cells, [far_in[2, f, j] for f in range(NF)], lane, 1)
+            u = conserved_of(cells)
+            for f in range(NF):
+                total = pltpu.roll(flux[f], NZ - 1, 0) - flux[f] + part[f] + (ext_flux[f, j + 1] - ext_flux[f, j])
+                u[f] = u[f] - (0.5 * time_step) * total
+            mid = primitive_of(u)
+            mid[2] = mid[2] - plane_kick
+            at = jnp.where(rad == 0, 0, 10)
+            for f in range(NF):
+                w[f, at + j] = mid[f]
+            return carry
+
+        lax.fori_loop(0, 2, row, 0)
+
     def receive_x(sec, w):
-        for side in range(2):
-            pltpu.make_async_copy(ghost.at[sec, side], ghost.at[sec, side], x_recv.at[sec, side]).wait()
-            for f in range(NF):
-                for j in range(2):
-                    value = ghost[sec, side, f, j]
-                    if f == 2:
-                        value = value + kick[side]
-                    w[f, j + (10 if side else 0)] = value
+        if sec == 0:
+            receive_side(0, w, 0)
+            receive_side(0, w, 1)
+            return
+
+        @pl.when(rad > 0)
+        def _():
+            receive_side(1, w, 0)
+
+        @pl.when(rad < RAD - 1)
+        def _():
+            receive_side(1, w, 1)
+
+        @pl.when(edge)
+        def _():
+            sheared_rows(w)
 
     def row_total(x):
         return [-0.5 * (acc[f, x] + (fx[f, x + 1] - fx[f, x])) for f in range(NF)]
@@ -296,17 +424,20 @@
             out_rows[pl.ds(f * NZ * NX + x, NZ, NX), :] = 0.5 * (tend[f, x] + total[f])
         return carry
 
+    scatter()
     for sec, w, end in ((0, w1, middle), (1, w2, last)):
         start_x(sec, w)
         start_y(sec, w)
         inside(w)
-        x_faces(w, 2, 7)
-        serve(sec)
+        x_faces(w, fx, 2, 7)
         finish_y(sec)
         lax.fori_loop(2, 6, end, 0)
+        if sec == 0:
+            load_shift.wait()
+            serve()
         receive_x(sec, w)
-        x_faces(w, 0, 2)
-        x_faces(w, 7, 9)
+        x_faces(w, fx, 0, 2)
+        x_faces(w, fx, 7, 9)
         lax.fori_loop(0, 2, end, 0)
         lax.fori_loop(6, 8, end, 0)
 
@@ -322,13 +453,15 @@
         def _():
             x_copy(sec, w, False).wait_send()
 
-        @pl.when(edge)
-        def _():
-            pltpu.make_async_copy(relay_in.at[sec], relay_in.at[sec], a_send.at[sec]).wait()
-
-        @pl.when(relay)
-        def _():
-            pltpu.make_async_copy(relay_out.at[sec], relay_out.at[sec], b_send.at[sec]).wait()
+    @pl.when(edge)
+    def _():
+        pltpu.make_async_copy(stage, stage, a_send).wait()
+
+    @pl.when(relay)
+    def _():
+        pltpu.make_async_copy(near_out, near_out, b_send).wait()
+        pltpu.make_async_copy(far_out, far_out, far_send).wait()
+        pltpu.make_async_copy(plane_out, plane_out, plane_send).wait()
 
 
 def shards(conserved, shear_shift):
@@ -336,7 +469,7 @@
     return pl.pallas_call(
         kernel,
         out_shape=jax.ShapeDtypeStruct((NF, NZ, NX, NY), f32),
-        in_specs=[pl.BlockSpec(memory_space=pltpu.SMEM), pl.BlockSpec(memory_space=pl.ANY)],
+        in_specs=[pl.BlockSpec(memory_space=pltpu.HBM), pl.BlockSpec(memory_space=pltpu.HBM)],
         out_specs=pl.BlockSpec(memory_space=pltpu.VMEM),
         scratch_shapes=[
             pltpu.VMEM((NF, NZ, NX, NY), f32),
@@ -350,17 +483,30 @@
             pltpu.VMEM((2, NF, NZ, NY), f32),
             pltpu.VMEM((2, NF, NZ, NY), f32),
             pltpu.VMEM((2, 2, NF, 2, NZ, NY), f32),
+            pltpu.VMEM((AZ, 2, 8, NY), f32),
+            pltpu.VMEM((AZ, 2, 8, NY), f32),
             pltpu.VMEM((2, AZ, 8, NY), f32),
             pltpu.VMEM((AZ, 8, NY), f32),
-            pltpu.VMEM((2, AZ, 8, NY), f32),
+            pltpu.VMEM((AZ, 3, 8, NY), f32),
+            pltpu.VMEM((AZ, 8, NY), f32),
+            pltpu.VMEM((3, NF, 2, NZ, NY), f32),
+            pltpu.VMEM((NF, 2, NZ, NY), f32),
+            pltpu.VMEM((NF, 6, NZ, NY), f32),
+            pltpu.VMEM((NF, 3, NZ, NY), f32),
+            pltpu.SMEM((2,), jnp.int32),
+            pltpu.SemaphoreType.DMA,
             pltpu.SemaphoreType.DMA,
             pltpu.SemaphoreType.DMA((2, 2)),
             pltpu.SemaphoreType.DMA((2, 2)),
             pltpu.SemaphoreType.DMA((2, 2)),
             pltpu.SemaphoreType.DMA((2, 2)),
-            pltpu.SemaphoreType.DMA((2,)),
-            pltpu.SemaphoreType.DMA((2,)),
-            pltpu.SemaphoreType.DMA((2,)),
+            pltpu.SemaphoreType.DMA,
+            pltpu.SemaphoreType.DMA,
+            pltpu.SemaphoreType.DMA,
+            pltpu.SemaphoreType.DMA,
+            pltpu.SemaphoreType.DMA,
+            pltpu.SemaphoreType.DMA,
+            pltpu.SemaphoreType.DMA,
         ],
         name="mhd_step",
         compiler_params=pltpu.CompilerParams(

time: 50.5 us -> 44.8 us (0.89)
  the two profiles are of different devices: /device:TPU:1 before, /device:TPU:0 now
where the time goes in v2:
time: 44.8 us; the launch traced here: 44.7 us
  Pallas kernels  42.2 us (94%)
  local copies, waits for them, and re-layouts  2.49 us (6%)
    pallas_call x1, Pallas kernels, shards(): pl.pallas_call(kernel, out_shape=jax.ShapeDtypeStruct((NF, NZ, NX, NY), f...  42.2 us
    unnamed x5, local copies, waits for them, and re-layouts  2.49 us

profile of v2, /device:TPU:0, one launch (start us, length us, event | category | flops | bytes accessed | tf_op | source)
XLA Modules:
  0.0 44.7 jit_solution(12330253021537958681)
XLA Ops:
  0.0 0.0 copy-start
  0.0 1.0 %copy-done = f32[8,16,8,128]{3,2,1,0:T(8,128)S(1)} copy-done((f32[8,16,8,128]{3,2,1,0:T(8,128)S(1)}, f32[8,16,8,128]{3,2,1,0:T(8,128)}, u32[]{:S(2)}) %copy-start) | copy-done | bytes 524312
  1.0 0.0 copy-start.1
  1.0 0.7 %copy-done.1 = s32[2]{0:T(128)S(1)} copy-done((s32[2]{0:T(128)S(1)}, s32[2]{0:T(128)}, u32[]{:S(2)}) %copy-start.1) | copy-done | bytes 32
  1.7 42.2 %mhd_step.1 = f32[8,16,8,128]{3,2,1,0:T(8,128)S(1)} custom-call(s32[2]{0:T(128)S(1)} %copy-done.1, f32[8,16,8,128]{3,2,1,0:T(8,128)S(1)} %copy-done), custom_call_target="tpu_custom_call" | custom-call | tf_op jit(solution)/shard_map/mhd_step/pallas_call | solution.py:469
  43.9 0.8 %copy.4 = f32[8,16,8,128]{3,2,1,0:T(8,128)} copy(f32[8,16,8,128]{3,2,1,0:T(8,128)S(1)} %mhd_step.1) | data formatting | bytes 1048576
Async XLA Ops:
  0.0 1.0 %copy-start = (f32[8,16,8,128]{3,2,1,0:T(8,128)S(1)}, f32[8,16,8,128]{3,2,1,0:T(8,128)}, u32[]{:S(2)}) copy-start(f32[8,16,8,128]{3,2,1,0:T(8,128)} %u_hbm.1) | copy-start | bytes 1572868
  1.0 0.7 %copy-start.1 = (s32[2]{0:T(128)S(1)}, s32[2]{0:T(128)}, u32[]{:S(2)}) copy-start(s32[2]{0:T(128)} %shift_hbm.1) | copy-start | bytes 28

commit v3 on v2

--- a/solution.py
+++ b/solution.py
@@ -98,17 +98,21 @@
             for f in range(NF)]
 
 
-def kernel(shift_hbm, u_hbm, out_ref, raw, w1, w2, acc, fx, tend, corr, strips, y_lo, y_hi, ghost, stage, relay_in,
+def plane_of(p):
+    return ((p // 2) % 4 + p // 8 + 2 * (p % 2)) % 4
+
+
+def kernel(shift_hbm, u_hbm, out_ref, raw, w1, w2, acc, fx, tend, wt, ft, y_out, y_in, ghost, stage, relay_in,
            relay_roll, near_out, far_out, plane_out, far_in, plane_in, ext_rows, ext_flux, shift_ref, in_sem, shift_sem,
            x_send, x_recv, y_send, y_recv, a_send, a_recv, b_send, far_send, far_recv, plane_send, plane_recv):
     az = lax.axis_index("az")
     rad = lax.axis_index("rad")
     right, left = (az + 1) % AZ, (az + AZ - 1) % AZ
     edge = (rad == 0) | (rad == RAD - 1)
-    relay_lo = rad == 4 + az % 3
-    relay_hi = rad == 3 - az % 3
+    relay_lo = rad == 4 + plane_of(az)
+    relay_hi = rad == 3 - plane_of(az)
     relay = relay_lo | relay_hi
-    kick = [jnp.where(rad == 0, shear_jump, 0.0), jnp.where(rad == RAD - 1, -shear_jump, 0.0)]
+    both = edge & relay
 
     barrier = pltpu.get_barrier_semaphore()
 
@@ -120,14 +124,20 @@
     load_shift = pltpu.make_async_copy(shift_hbm, shift_ref, shift_sem)
     load_shift.start()
 
+    def others(body):
+        @pl.when(jnp.logical_not(both))
+        def _():
+            body(az)
+
+        def step(k, carry):
+            body((k + az) % AZ)
+            return carry
+
+        lax.fori_loop(1, AZ, step, 0)
+
     @pl.when(relay)
     def _():
-        source = jnp.where(relay_lo, RAD - 1, 0)
-
-        def step(k, carry):
-            signal((k + az) % AZ, source)
-            return carry
-        lax.fori_loop(0, AZ, step, 0)
+        others(lambda p: signal(p, jnp.where(relay_lo, RAD - 1, 0)))
 
     signal(right, rad)
     signal(left, rad)
@@ -142,19 +152,16 @@
 
     @pl.when(edge)
     def _():
+        others(lambda p: signal(p, jnp.where(rad == 0, 3 - plane_of(p), 4 + plane_of(p))))
+
         def step(k, carry):
             p = (k + az) % AZ
-            signal(p, 4 + p % 3)
-            signal(p, 3 - p % 3)
-            return carry
+            signal(p, jnp.where(rad == 0, 4 + plane_of(p), 3 - plane_of(p)))
+            return carry
+
         lax.fori_loop(0, AZ, step, 0)
 
     lane = lax.broadcasted_iota(jnp.int32, (NZ, NY), 1)
-    slot = lane % 16
-    block = lane // 16
-    inner = (lane > 1) & (lane < NY - 1)
-    seam = (lane < 2) | (lane >= NY - 2)
-
     load.wait()
     u_rows = raw.reshape(NF * NZ * NX, NY)
 
@@ -168,6 +175,13 @@
         return carry
 
     lax.fori_loop(0, NX, first_rows, 0)
+
+    def turn_y(sec, w):
+        for f in range(NF):
+            wt[f, 8:8 + NY] = w[f, 2:2 + NX].reshape(NX * NZ, NY).T
+        for f in range(NF):
+            y_out[sec, 0, 2 * f:2 * f + 2] = wt[f, 8 + NY - 2:8 + NY]
+            y_out[sec, 1, 2 * f:2 * f + 2] = wt[f, 8:10]
 
     @pl.when(edge)
     def _():
@@ -179,7 +193,8 @@
                     for half in range(2):
                         stage[f * 4 + j * 2 + half, t] = row[half * 8:half * 8 + 8]
 
-    pl.semaphore_wait(barrier, jnp.where(edge, AZ + 3, jnp.where(relay, 2 * AZ + 4, 4)))
+    turn_y(0, w1)
+    pl.semaphore_wait(barrier, jnp.where(edge, AZ + 3, 4) + jnp.where(relay, 2 * AZ, 0) - jnp.where(both, 2, 0))
 
     def x_copy(sec, w, up):
         rows = w.at[:, pl.ds(8 if up else 2, 2)]
@@ -189,22 +204,24 @@
             device_id=(az, rad + 1 if up else rad - 1), device_id_type=MESH)
 
     def y_copy(sec, up):
+        side = 0 if up else 1
         return pltpu.make_async_remote_copy(
-            strips.at[sec], (y_lo if up else y_hi).at[sec], y_send.at[sec, 0 if up else 1],
-            y_recv.at[sec, 0 if up else 1],
+            y_out.at[sec, side], y_in.at[sec, side], y_send.at[sec, side], y_recv.at[sec, side],
             device_id=(right if up else left, rad), device_id_type=MESH)
 
     def scatter():
         @pl.when(edge)
         def _():
-            def step(k, carry):
-                p = (k + az) % AZ
+            def send(p):
                 pltpu.make_async_remote_copy(
                     stage.at[p], relay_in.at[az], a_send, a_recv,
-                    device_id=(p, jnp.where(rad == 0, 3 - p % 3, 4 + p % 3)), device_id_type=MESH).start()
-                return carry
-
-            lax.fori_loop(0, AZ, step, 0)
+                    device_id=(p, jnp.where(rad == 0, 3 - plane_of(p), 4 + plane_of(p))), device_id_type=MESH).start()
+
+            others(send)
+
+            @pl.when(both)
+            def _():
+                pltpu.make_async_copy(stage.at[az], relay_in.at[az], a_recv).start()
 
     def start_x(sec, w):
         @pl.when(rad < RAD - 1)
@@ -215,13 +232,7 @@
         def _():
             x_copy(sec, w, False).start()
 
-    def start_y(sec, w):
-        for f in range(NF):
-            q = w[f, 2]
-            q = pltpu.roll(q, 8, 1)
-            for x in range(1, NX):
-                q = jnp.where(block == x, pltpu.roll(w[f, x + 2], (16 * x + 8) % NY, 1), q)
-            strips[sec, f] = q
+    def start_y(sec):
         y_copy(sec, True).start()
         y_copy(sec, False).start()
 
@@ -242,12 +253,9 @@
             def turn(slots, tiles, amount):
                 part = amount % NY
 
-                def step(k, carry):
+                for k in range(AZ):
                     for c, t in zip(slots, tiles):
                         relay_roll[c, k] = pltpu.roll(relay_in[k, t], (NY - part) % NY, 1)
-                    return carry
-
-                lax.fori_loop(0, AZ, step, 0, unroll=4)
 
             def pick(c, d, amount):
                 whole, part = amount // NY, amount % NY
@@ -264,7 +272,7 @@
                     device_id=(d, across), device_id_type=MESH).start()
                 return carry
 
-            lax.fori_loop(0, AZ, near_step, 0)
+            lax.fori_loop(0, AZ, near_step, 0, unroll=4)
             turn((0, 1), (0, 1), shift_1)
 
             def pick_step(d, carry):
@@ -272,7 +280,7 @@
                     far_out[d, t] = pick(t, d, shift_1)
                 return carry
 
-            lax.fori_loop(0, AZ, pick_step, 0)
+            lax.fori_loop(0, AZ, pick_step, 0, unroll=8)
 
             def far_step(k, carry):
                 d = (k + az) % AZ
@@ -282,33 +290,54 @@
                     device_id=(d, across), device_id_type=MESH).start()
                 return carry
 
-            lax.fori_loop(0, AZ, far_step, 0)
+            lax.fori_loop(0, AZ, far_step, 0, unroll=4)
             shift_2 = (shift_0 - shift_1 + COLS) % COLS
             turn((0,), (0,), shift_2)
 
-            def plane_step(k, carry):
-                d = (k + az) % AZ
+            def plane_step(d, carry):
                 plane_out[d] = pick(0, d, shift_2)
+                return carry
+
+            lax.fori_loop(0, AZ, plane_step, 0, unroll=8)
+
+            def send(d):
                 pltpu.make_async_remote_copy(
                     plane_out.at[d], plane_in.at[f, j, rows], plane_send, plane_recv,
                     device_id=(d, RAD - 1 - across), device_id_type=MESH).start()
-                return carry
-
-            lax.fori_loop(0, AZ, plane_step, 0)
-
-    def inside(w):
+
+            others(send)
+
+            @pl.when(both)
+            def _():
+                pltpu.make_async_copy(plane_out.at[az], plane_in.at[f, j, rows], plane_recv).start()
+
+    def z_part(w):
         def row(x, carry):
-            cells = [w[f, x + 2] for f in range(NF)]
-            flux = rolled_faces(cells, 0, 2)
+            flux = rolled_faces([w[f, x + 2] for f in range(NF)], 0, 2)
             for f in range(NF):
                 acc[f, x] = pltpu.roll(flux[f], NZ - 1, 0) - flux[f]
-            flux = rolled_faces(cells, 1, 1)
-            for f in range(NF):
-                masked = jnp.where(inner, flux[f], 0.0)
-                acc[f, x] += pltpu.roll(masked, NY - 1, 1) - masked
             return carry
 
         lax.fori_loop(0, NX, row, 0)
+
+    def y_faces(k):
+        lefts, rights = [], []
+        for f in range(NF):
+            c = [wt[f, pl.ds(8 * k + 6 + o, 8)] for o in range(4)]
+            d = [c[o + 1] - c[o] for o in range(3)]
+            lefts.append(c[1] + half_slope(d[0], d[1]))
+            rights.append(c[2] - half_slope(d[1], d[2]))
+        flux = twice_flux(lefts, rights, 1)
+        for f in range(NF):
+            ft[f, pl.ds(pl.multiple_of(8 * k, 8), 8)] = flux[f]
+
+    def y_part():
+        def pair(k, carry):
+            y_faces(2 * k + 1)
+            y_faces(2 * k + 2)
+            return carry
+
+        lax.fori_loop(0, 7, pair, 0)
 
     def x_faces(w, flux_ref, begin, end):
         def face(i, carry):
@@ -328,31 +357,23 @@
     def finish_y(sec):
         y_copy(sec, True).wait_recv()
         y_copy(sec, False).wait_recv()
-        cells = []
-        for f in range(NF):
-            own = strips[sec, f]
-            lower = jnp.where((slot >= 4) & (slot < 8), y_lo[sec, f], own)
-            upper = jnp.where((slot >= 8) & (slot < 12), y_hi[sec, f], own)
-            cells.append(jnp.where(slot < 8, pltpu.roll(lower, NY - 4, 1), pltpu.roll(upper, 4, 1)))
-        flux = rolled_faces(cells, 1, 1)
-        for f in range(NF):
-            masked = jnp.where((slot == 4) | (slot == 5) | (slot == 11) | (slot == 12), flux[f], 0.0)
-            d = pltpu.roll(masked, NY - 1, 1) - masked
-            far = pltpu.roll(d, NY - 8, 1)
-            corr[f] = jnp.where((slot == 4) | (slot == 5), d, jnp.where((slot == 2) | (slot == 3), far, 0.0))
-        for f in range(NF):
-            value = corr[f]
-            for x in range(NX):
-                acc[f, x] += jnp.where(seam, pltpu.roll(value, (124 - 16 * x) % NY, 1), 0.0)
+        for f in range(NF):
+            wt[f, 6:8] = y_in[sec, 0, 2 * f:2 * f + 2]
+            wt[f, 8 + NY:10 + NY] = y_in[sec, 1, 2 * f:2 * f + 2]
+        for k in (0, 15, 16):
+            y_faces(k)
+        for f in range(NF):
+            part = (ft[f, 1:NY + 1] - ft[f, 0:NY]).T
+            acc[f] += part.reshape(NX, NZ, NY)
 
     def receive_side(sec, w, side):
         pltpu.make_async_copy(ghost.at[sec, side], ghost.at[sec, side], x_recv.at[sec, side]).wait()
+        kick = jnp.where((rad == 0) & (side == 0), shear_jump, 0.0) - jnp.where(
+            (rad == RAD - 1) & (side == 1), shear_jump, 0.0)
         for f in range(NF):
             for j in range(2):
                 value = ghost[sec, side, f, j]
-                if f == 2:
-                    value = value + kick[side]
-                w[f, j + (10 if side else 0)] = value
+                w[f, 10 * side + j] = value + kick if f == 2 else value
 
     def sheared_rows(w):
         pltpu.make_async_copy(plane_in, plane_in, plane_recv).wait()
@@ -386,23 +407,27 @@
 
         lax.fori_loop(0, 2, row, 0)
 
-    def receive_x(sec, w):
-        if sec == 0:
-            receive_side(0, w, 0)
-            receive_side(0, w, 1)
-            return
-
-        @pl.when(rad > 0)
-        def _():
-            receive_side(1, w, 0)
-
-        @pl.when(rad < RAD - 1)
-        def _():
-            receive_side(1, w, 1)
-
-        @pl.when(edge)
-        def _():
-            sheared_rows(w)
+    def sides(sec, w, end):
+        def step(k, carry):
+            side = (k + jnp.where(rad == 0, 1, 0)) % 2
+            if sec == 0:
+                receive_side(sec, w, side)
+            else:
+                sheared = edge & (k == 1)
+
+                @pl.when(sheared)
+                def _():
+                    sheared_rows(w)
+
+                @pl.when(jnp.logical_not(sheared))
+                def _():
+                    receive_side(sec, w, side)
+
+            x_faces(w, fx, 7 * side, 7 * side + 2)
+            lax.fori_loop(6 * side, 6 * side + 2, end, 0)
+            return carry
+
+        lax.fori_loop(0, 2, step, 0)
 
     def row_total(x):
         return [-0.5 * (acc[f, x] + (fx[f, x + 1] - fx[f, x])) for f in range(NF)]
@@ -427,19 +452,18 @@
     scatter()
     for sec, w, end in ((0, w1, middle), (1, w2, last)):
         start_x(sec, w)
-        start_y(sec, w)
-        inside(w)
+        if sec == 1:
+            turn_y(sec, w)
+        start_y(sec)
+        z_part(w)
+        y_part()
         x_faces(w, fx, 2, 7)
         finish_y(sec)
         lax.fori_loop(2, 6, end, 0)
         if sec == 0:
             load_shift.wait()
             serve()
-        receive_x(sec, w)
-        x_faces(w, fx, 0, 2)
-        x_faces(w, fx, 7, 9)
-        lax.fori_loop(0, 2, end, 0)
-        lax.fori_loop(6, 8, end, 0)
+        sides(sec, w, end)
 
     for sec, w in ((0, w1), (1, w2)):
         y_copy(sec, True).wait_send()
@@ -455,13 +479,23 @@
 
     @pl.when(edge)
     def _():
-        pltpu.make_async_copy(stage, stage, a_send).wait()
+        most = stage.at[pl.ds(0, AZ - 1)]
+        pltpu.make_async_copy(most, most, a_send).wait()
+
+        @pl.when(jnp.logical_not(relay))
+        def _():
+            pltpu.make_async_copy(stage.at[0], stage.at[0], a_send).wait()
 
     @pl.when(relay)
     def _():
         pltpu.make_async_copy(near_out, near_out, b_send).wait()
         pltpu.make_async_copy(far_out, far_out, far_send).wait()
-        pltpu.make_async_copy(plane_out, plane_out, plane_send).wait()
+        most = plane_out.at[pl.ds(0, AZ - 1)]
+        pltpu.make_async_copy(most, most, plane_send).wait()
+
+        @pl.when(jnp.logical_not(edge))
+        def _():
+            pltpu.make_async_copy(plane_out.at[0], plane_out.at[0], plane_send).wait()
 
 
 def shards(conserved, shear_shift):
@@ -478,10 +512,10 @@
             pltpu.VMEM((NF, NX, NZ, NY), f32),
             pltpu.VMEM((NF, NX + 1, NZ, NY), f32),
             pltpu.VMEM((NF, NX, NZ, NY), f32),
-            pltpu.VMEM((NF, NZ, NY), f32),
-            pltpu.VMEM((2, NF, NZ, NY), f32),
-            pltpu.VMEM((2, NF, NZ, NY), f32),
-            pltpu.VMEM((2, NF, NZ, NY), f32),
+            pltpu.VMEM((NF, NY + 24, NX * NZ), f32),
+            pltpu.VMEM((NF, NY + 8, NX * NZ), f32),
+            pltpu.VMEM((2, 2, 2 * NF, NX * NZ), f32),
+            pltpu.VMEM((2, 2, 2 * NF, NX * NZ), f32),
             pltpu.VMEM((2, 2, NF, 2, NZ, NY), f32),
             pltpu.VMEM((AZ, 2, 8, NY), f32),
             pltpu.VMEM((AZ, 2, 8, NY), f32),
@@ -510,7 +544,7 @@
         ],
         name="mhd_step",
         compiler_params=pltpu.CompilerParams(
-            collective_id=0, has_side_effects=True, vmem_limit_bytes=32 * 1024 * 1024),
+            collective_id=0, has_side_effects=True, vmem_limit_bytes=53 * 1024 * 1024),
     )(shear_shift, conserved)
 
 

time: 44.8 us -> 39 us (0.87)
  the two profiles are of different devices: /device:TPU:0 before, /device:TPU:1 now
where the time goes in v3:
time: 39 us; the launch traced here: 38.3 us
  Pallas kernels  36.8 us (94%)
  local copies, waits for them, and re-layouts  1.45 us (4%)
    pallas_call x1, Pallas kernels, shards(): pl.pallas_call(kernel, out_shape=jax.ShapeDtypeStruct((NF, NZ, NX, NY), f...  36.8 us
    unnamed x3, local copies, waits for them, and re-layouts  1.45 us

profile of v3, /device:TPU:1, one launch (start us, length us, event | category | flops | bytes accessed | tf_op | source)
XLA Modules:
  0.0 38.3 jit_solution(7962587971081144783)
XLA Ops:
  0.0 0.0 copy-start
  0.0 0.7 %copy-done = s32[2]{0:T(128)S(1)} copy-done((s32[2]{0:T(128)S(1)}, s32[2]{0:T(128)}, u32[]{:S(2)}) %copy-start) | copy-done | bytes 32
  0.7 36.8 %mhd_step.1 = f32[8,16,8,128]{3,2,1,0:T(8,128)S(1)} custom-call(s32[2]{0:T(128)S(1)} %copy-done, f32[8,16,8,128]{3,2,1,0:T(8,128)} %u_hbm.1), custom_call_target="tpu_custom_call" | custom-call | tf_op jit(solution)/shard_map/mhd_step/pallas_call | solution.py:503
  37.5 0.8 %copy.4 = f32[8,16,8,128]{3,2,1,0:T(8,128)} copy(f32[8,16,8,128]{3,2,1,0:T(8,128)S(1)} %mhd_step.1) | data formatting | bytes 1048576
Async XLA Ops:
  0.0 0.7 %copy-start = (s32[2]{0:T(128)S(1)}, s32[2]{0:T(128)}, u32[]{:S(2)}) copy-start(s32[2]{0:T(128)} %shift_hbm.1) | copy-start | bytes 28

commit v4 on v3

--- a/solution.py
+++ b/solution.py
@@ -99,7 +99,7 @@
 
 
 def plane_of(p):
-    return ((p // 2) % 4 + p // 8 + 2 * (p % 2)) % 4
+    return 3 - ((p // 2) % 4 + p // 8 + p % 2) % 3
 
 
 def kernel(shift_hbm, u_hbm, out_ref, raw, w1, w2, acc, fx, tend, wt, ft, y_out, y_in, ghost, stage, relay_in,
@@ -124,16 +124,26 @@
     load_shift = pltpu.make_async_copy(shift_hbm, shift_ref, shift_sem)
     load_shift.start()
 
+    def peer(k, across):
+        z, x, core = az // 8, (az // 2) % 4, az % 2
+        zi, xi = k // 8, (k // 2) % 4
+        if across:
+            zi = 3 - zi
+        z = jnp.where(zi == 0, 3 - z, jnp.where(zi == 1, (z + 2) % 4, jnp.where(zi == 2, z + 1 - 2 * (z % 2), z)))
+        x = (x + jnp.where(xi == 0, 2, jnp.where(xi == 3, 0, 2 * xi - 1))) % 4
+        core = jnp.where(k % 2 == 0, 1 - core, core)
+        return (z * 4 + x) * 2 + core
+
     def others(body):
+        def step(k, carry):
+            body(peer(k, False))
+            return carry
+
+        lax.fori_loop(0, AZ - 1, step, 0)
+
         @pl.when(jnp.logical_not(both))
         def _():
             body(az)
-
-        def step(k, carry):
-            body((k + az) % AZ)
-            return carry
-
-        lax.fori_loop(1, AZ, step, 0)
 
     @pl.when(relay)
     def _():
@@ -152,14 +162,7 @@
 
     @pl.when(edge)
     def _():
-        others(lambda p: signal(p, jnp.where(rad == 0, 3 - plane_of(p), 4 + plane_of(p))))
-
-        def step(k, carry):
-            p = (k + az) % AZ
-            signal(p, jnp.where(rad == 0, 4 + plane_of(p), 3 - plane_of(p)))
-            return carry
-
-        lax.fori_loop(0, AZ, step, 0)
+        signal(az, RAD - 1 - rad)
 
     lane = lax.broadcasted_iota(jnp.int32, (NZ, NY), 1)
     load.wait()
@@ -191,10 +194,10 @@
                 for t, base in ((0, near), (1, far)):
                     row = w1[f, base + j]
                     for half in range(2):
-                        stage[f * 4 + j * 2 + half, t] = row[half * 8:half * 8 + 8]
+                        stage[t, f * 4 + j * 2 + half] = row[half * 8:half * 8 + 8]
 
     turn_y(0, w1)
-    pl.semaphore_wait(barrier, jnp.where(edge, AZ + 3, 4) + jnp.where(relay, 2 * AZ, 0) - jnp.where(both, 2, 0))
+    pl.semaphore_wait(barrier, jnp.where(edge, AZ + 4, 4) - jnp.where(both, 1, 0))
 
     def x_copy(sec, w, up):
         rows = w.at[:, pl.ds(8 if up else 2, 2)]
@@ -212,23 +215,24 @@
     def scatter():
         @pl.when(edge)
         def _():
-            def send(p):
-                pltpu.make_async_remote_copy(
-                    stage.at[p], relay_in.at[az], a_send, a_recv,
-                    device_id=(p, jnp.where(rad == 0, 3 - plane_of(p), 4 + plane_of(p))), device_id_type=MESH).start()
-
-            others(send)
-
-            @pl.when(both)
-            def _():
-                pltpu.make_async_copy(stage.at[az], relay_in.at[az], a_recv).start()
-
-    def start_x(sec, w):
-        @pl.when(rad < RAD - 1)
+            for t in range(2):
+                def send(p):
+                    pltpu.make_async_remote_copy(
+                        stage.at[t, p], relay_in.at[t, az], a_send.at[t], a_recv.at[t],
+                        device_id=(p, jnp.where(rad == 0, 3 - plane_of(p), 4 + plane_of(p))), device_id_type=MESH).start()
+
+                others(send)
+
+                @pl.when(both)
+                def _():
+                    pltpu.make_async_copy(stage.at[t, az], relay_in.at[t, az], a_recv.at[t]).start()
+
+    def start_x(sec, w, side):
+        @pl.when((side == 1) & (rad < RAD - 1))
         def _():
             x_copy(sec, w, True).start()
 
-        @pl.when(rad > 0)
+        @pl.when((side == 0) & (rad > 0))
         def _():
             x_copy(sec, w, False).start()
 
@@ -248,24 +252,27 @@
             side = jnp.where(relay_lo, 0, 1)
             across = jnp.where(relay_lo, 0, RAD - 1)
             small = lax.broadcasted_iota(jnp.int32, (8, NY), 1)
-            pltpu.make_async_copy(relay_in, relay_in, a_recv).wait()
+
+            def arrived(t):
+                pltpu.make_async_copy(relay_in.at[t], relay_in.at[t], a_recv.at[t]).wait()
 
             def turn(slots, tiles, amount):
                 part = amount % NY
 
                 for k in range(AZ):
                     for c, t in zip(slots, tiles):
-                        relay_roll[c, k] = pltpu.roll(relay_in[k, t], (NY - part) % NY, 1)
+                        relay_roll[c, k] = pltpu.roll(relay_in[t, k], (NY - part) % NY, 1)
 
             def pick(c, d, amount):
                 whole, part = amount // NY, amount % NY
                 return jnp.where(
                     small < NY - part, relay_roll[c, (d + whole) % AZ], relay_roll[c, (d + whole + 1) % AZ])
 
+            arrived(0)
             turn((0,), (0,), shift_0)
 
             def near_step(k, carry):
-                d = (k + az) % AZ
+                d = peer(k, True)
                 near_out[d] = pick(0, d, shift_0)
                 pltpu.make_async_remote_copy(
                     near_out.at[d], ghost.at[0, side, f, j, rows], b_send, x_recv.at[0, side],
@@ -273,7 +280,9 @@
                 return carry
 
             lax.fori_loop(0, AZ, near_step, 0, unroll=4)
-            turn((0, 1), (0, 1), shift_1)
+            turn((0,), (0,), shift_1)
+            arrived(1)
+            turn((1,), (1,), shift_1)
 
             def pick_step(d, carry):
                 for t in range(2):
@@ -283,7 +292,7 @@
             lax.fori_loop(0, AZ, pick_step, 0, unroll=8)
 
             def far_step(k, carry):
-                d = (k + az) % AZ
+                d = peer(k, True)
                 far_out[d, 2] = jnp.where(small < NY // 2, far_out[(d + 1) % AZ, 0], far_out[(d + AZ - 1) % AZ, 0])
                 pltpu.make_async_remote_copy(
                     far_out.at[d], far_in.at[:, f, j, rows], far_send, far_recv,
@@ -390,7 +399,8 @@
                 ext_rows[f, 4 - far_at + j] = value
         x_faces(ext_rows, ext_flux, 0, 3)
 
-        def row(j, carry):
+        at = jnp.where(rad == 0, 0, 10)
+        for j in range(2):
             cells = [ext_rows[f, 2 + j] for f in range(NF)]
             flux = rolled_faces(cells, 0, 2)
             part = ghosted_divergence(cells, [far_in[2, f, j] for f in range(NF)], lane, 1)
@@ -400,34 +410,14 @@
                 u[f] = u[f] - (0.5 * time_step) * total
             mid = primitive_of(u)
             mid[2] = mid[2] - plane_kick
-            at = jnp.where(rad == 0, 0, 10)
             for f in range(NF):
                 w[f, at + j] = mid[f]
-            return carry
-
-        lax.fori_loop(0, 2, row, 0)
-
-    def sides(sec, w, end):
-        def step(k, carry):
-            side = (k + jnp.where(rad == 0, 1, 0)) % 2
-            if sec == 0:
-                receive_side(sec, w, side)
-            else:
-                sheared = edge & (k == 1)
-
-                @pl.when(sheared)
-                def _():
-                    sheared_rows(w)
-
-                @pl.when(jnp.logical_not(sheared))
-                def _():
-                    receive_side(sec, w, side)
-
-            x_faces(w, fx, 7 * side, 7 * side + 2)
-            lax.fori_loop(6 * side, 6 * side + 2, end, 0)
-            return carry
-
-        lax.fori_loop(0, 2, step, 0)
+
+    def side_at(k):
+        return (k + jnp.where(rad == 0, 1, 0)) % 2
+
+    def side_faces(w, side):
+        x_faces(w, fx, 7 * side, 7 * side + 2)
 
     def row_total(x):
         return [-0.5 * (acc[f, x] + (fx[f, x + 1] - fx[f, x])) for f in range(NF)]
@@ -449,21 +439,52 @@
             out_rows[pl.ds(f * NZ * NX + x, NZ, NX), :] = 0.5 * (tend[f, x] + total[f])
         return carry
 
-    scatter()
-    for sec, w, end in ((0, w1, middle), (1, w2, last)):
-        start_x(sec, w)
-        if sec == 1:
-            turn_y(sec, w)
-        start_y(sec)
+    def bulk(w):
         z_part(w)
         y_part()
         x_faces(w, fx, 2, 7)
-        finish_y(sec)
-        lax.fori_loop(2, 6, end, 0)
-        if sec == 0:
-            load_shift.wait()
-            serve()
-        sides(sec, w, end)
+
+    scatter()
+    start_y(0)
+    bulk(w1)
+    finish_y(0)
+    lax.fori_loop(2, 6, middle, 0)
+    start_x(0, w1, 0)
+    start_x(0, w1, 1)
+    load_shift.wait()
+    serve()
+
+    def first_side(k, carry):
+        side = side_at(k)
+        receive_side(0, w1, side)
+        side_faces(w1, side)
+        lax.fori_loop(6 * side, 6 * side + 2, middle, 0)
+        start_x(1, w2, side)
+        return carry
+
+    lax.fori_loop(0, 2, first_side, 0)
+    turn_y(1, w2)
+    start_y(1)
+    bulk(w2)
+
+    def second_side(k, carry):
+        side = side_at(k)
+        sheared = edge & (k == 1)
+
+        @pl.when(sheared)
+        def _():
+            sheared_rows(w2)
+
+        @pl.when(jnp.logical_not(sheared))
+        def _():
+            receive_side(1, w2, side)
+
+        side_faces(w2, side)
+        return carry
+
+    lax.fori_loop(0, 2, second_side, 0)
+    finish_y(1)
+    lax.fori_loop(0, NX, last, 0)
 
     for sec, w in ((0, w1), (1, w2)):
         y_copy(sec, True).wait_send()
@@ -479,12 +500,13 @@
 
     @pl.when(edge)
     def _():
-        most = stage.at[pl.ds(0, AZ - 1)]
-        pltpu.make_async_copy(most, most, a_send).wait()
-
-        @pl.when(jnp.logical_not(relay))
-        def _():
-            pltpu.make_async_copy(stage.at[0], stage.at[0], a_send).wait()
+        for t in range(2):
+            most = stage.at[t, pl.ds(0, AZ - 1)]
+            pltpu.make_async_copy(most, most, a_send.at[t]).wait()
+
+            @pl.when(jnp.logical_not(relay))
+            def _():
+                pltpu.make_async_copy(stage.at[t, 0], stage.at[t, 0], a_send.at[t]).wait()
 
     @pl.when(relay)
     def _():
@@ -517,8 +539,8 @@
             pltpu.VMEM((2, 2, 2 * NF, NX * NZ), f32),
             pltpu.VMEM((2, 2, 2 * NF, NX * NZ), f32),
             pltpu.VMEM((2, 2, NF, 2, NZ, NY), f32),
-            pltpu.VMEM((AZ, 2, 8, NY), f32),
-            pltpu.VMEM((AZ, 2, 8, NY), f32),
+            pltpu.VMEM((2, AZ, 8, NY), f32),
+            pltpu.VMEM((2, AZ, 8, NY), f32),
             pltpu.VMEM((2, AZ, 8, NY), f32),
             pltpu.VMEM((AZ, 8, NY), f32),
             pltpu.VMEM((AZ, 3, 8, NY), f32),
@@ -534,8 +556,8 @@
             pltpu.SemaphoreType.DMA((2, 2)),
             pltpu.SemaphoreType.DMA((2, 2)),
             pltpu.SemaphoreType.DMA((2, 2)),
-            pltpu.SemaphoreType.DMA,
-            pltpu.SemaphoreType.DMA,
+            pltpu.SemaphoreType.DMA((2,)),
+            pltpu.SemaphoreType.DMA((2,)),
             pltpu.SemaphoreType.DMA,
             pltpu.SemaphoreType.DMA,
             pltpu.SemaphoreType.DMA,

time: 39 us -> 37.8 us (0.969); the launches traced: 38.3 us -> 37.7 us
  Pallas kernels: 36.8 us -> 36.2 us
    pallas_call x1, Pallas kernels: 36.8 us -> 36.2 us  [shards(): pl.pallas_call(kernel, out_shape=jax.ShapeDtypeStruct((NF, NZ, NX, NY), f...]
where the time goes in v4:
time: 37.8 us; the launch traced here: 37.7 us
  Pallas kernels  36.2 us (96%)
  local copies, waits for them, and re-layouts  1.45 us (4%)
    pallas_call x1, Pallas kernels, shards(): pl.pallas_call(kernel, out_shape=jax.ShapeDtypeStruct((NF, NZ, NX, NY), f...  36.2 us
    unnamed x3, local copies, waits for them, and re-layouts  1.45 us

profile of v4, /device:TPU:1, one launch (start us, length us, event | category | flops | bytes accessed | tf_op | source)
XLA Modules:
  0.0 37.7 jit_solution(10766899378925087713)
XLA Ops:
  0.0 0.0 copy-start
  0.0 0.7 %copy-done = s32[2]{0:T(128)S(1)} copy-done((s32[2]{0:T(128)S(1)}, s32[2]{0:T(128)}, u32[]{:S(2)}) %copy-start) | copy-done | bytes 32
  0.7 36.2 %mhd_step.1 = f32[8,16,8,128]{3,2,1,0:T(8,128)S(1)} custom-call(s32[2]{0:T(128)S(1)} %copy-done, f32[8,16,8,128]{3,2,1,0:T(8,128)} %u_hbm.1), custom_call_target="tpu_custom_call" | custom-call | tf_op jit(solution)/shard_map/mhd_step/pallas_call | solution.py:525
  36.9 0.8 %copy.4 = f32[8,16,8,128]{3,2,1,0:T(8,128)} copy(f32[8,16,8,128]{3,2,1,0:T(8,128)S(1)} %mhd_step.1) | data formatting | bytes 1048576
Async XLA Ops:
  0.0 0.7 %copy-start = (s32[2]{0:T(128)S(1)}, s32[2]{0:T(128)}, u32[]{:S(2)}) copy-start(s32[2]{0:T(128)} %shift_hbm.1) | copy-start | bytes 28

commit v5 on v4

--- a/solution.py
+++ b/solution.py
@@ -98,8 +98,9 @@
             for f in range(NF)]
 
 
-def plane_of(p):
-    return 3 - ((p // 2) % 4 + p // 8 + p % 2) % 3
+def plane_of(z, x, core):
+    s = z + x + core
+    return 3 - (s - 3 * ((s * 11) >> 5))
 
 
 def kernel(shift_hbm, u_hbm, out_ref, raw, w1, w2, acc, fx, tend, wt, ft, y_out, y_in, ghost, stage, relay_in,
@@ -109,8 +110,10 @@
     rad = lax.axis_index("rad")
     right, left = (az + 1) % AZ, (az + AZ - 1) % AZ
     edge = (rad == 0) | (rad == RAD - 1)
-    relay_lo = rad == 4 + plane_of(az)
-    relay_hi = rad == 3 - plane_of(az)
+    my_z, my_x, my_core = az >> 3, (az >> 1) & 3, az & 1
+    my_plane = plane_of(my_z, my_x, my_core)
+    relay_lo = rad == 4 + my_plane
+    relay_hi = rad == 3 - my_plane
     relay = relay_lo | relay_hi
     both = edge & relay
 
@@ -124,30 +127,31 @@
     load_shift = pltpu.make_async_copy(shift_hbm, shift_ref, shift_sem)
     load_shift.start()
 
-    def peer(k, across):
-        z, x, core = az // 8, (az // 2) % 4, az % 2
-        zi, xi = k // 8, (k // 2) % 4
-        if across:
-            zi = 3 - zi
-        z = jnp.where(zi == 0, 3 - z, jnp.where(zi == 1, (z + 2) % 4, jnp.where(zi == 2, z + 1 - 2 * (z % 2), z)))
-        x = (x + jnp.where(xi == 0, 2, jnp.where(xi == 3, 0, 2 * xi - 1))) % 4
-        core = jnp.where(k % 2 == 0, 1 - core, core)
-        return (z * 4 + x) * 2 + core
+    z_list = [3 - my_z, (my_z + 2) & 3, my_z + 1 - 2 * (my_z & 1), my_z]
+    x_list = [(my_x + 2) & 3, (my_x + 1) & 3, (my_x + 3) & 3, my_x]
+    core_list = [1 - my_core, my_core]
+
+    def peers(across):
+        out = []
+        for z in reversed(z_list) if across else z_list:
+            for x in x_list:
+                for core in core_list:
+                    out.append((z * 8 + x * 2 + core, plane_of(z, x, core)))
+        return out
 
     def others(body):
-        def step(k, carry):
-            body(peer(k, False))
-            return carry
-
-        lax.fori_loop(0, AZ - 1, step, 0)
+        everyone = peers(False)
+        for p, plane in everyone[:-1]:
+            body(p, plane)
 
         @pl.when(jnp.logical_not(both))
         def _():
-            body(az)
+            body(*everyone[-1])
 
     @pl.when(relay)
     def _():
-        others(lambda p: signal(p, jnp.where(relay_lo, RAD - 1, 0)))
+        source = jnp.where(relay_lo, RAD - 1, 0)
+        others(lambda p, plane: signal(p, source))
 
     signal(right, rad)
     signal(left, rad)
@@ -215,11 +219,12 @@
     def scatter():
         @pl.when(edge)
         def _():
+            base, sign = jnp.where(rad == 0, 3, 4), jnp.where(rad == 0, -1, 1)
             for t in range(2):
-                def send(p):
+                def send(p, plane):
                     pltpu.make_async_remote_copy(
                         stage.at[t, p], relay_in.at[t, az], a_send.at[t], a_recv.at[t],
-                        device_id=(p, jnp.where(rad == 0, 3 - plane_of(p), 4 + plane_of(p))), device_id_type=MESH).start()
+                        device_id=(p, base + sign * plane), device_id_type=MESH).start()
 
                 others(send)
 
@@ -247,7 +252,7 @@
                 return jnp.where(relay_lo, s, COLS - s) % COLS
 
             shift_0, shift_1 = signed(shift_ref[0]), signed(shift_ref[1])
-            f, j, half = az // 4, (az // 2) % 2, az % 2
+            f, j, half = az >> 2, (az >> 1) & 1, az & 1
             rows = pl.ds(pl.multiple_of(half * 8, 8), 8)
             side = jnp.where(relay_lo, 0, 1)
             across = jnp.where(relay_lo, 0, RAD - 1)
@@ -264,52 +269,47 @@
                         relay_roll[c, k] = pltpu.roll(relay_in[t, k], (NY - part) % NY, 1)
 
             def pick(c, d, amount):
-                whole, part = amount // NY, amount % NY
+                whole, part = amount >> 7, amount & (NY - 1)
                 return jnp.where(
-                    small < NY - part, relay_roll[c, (d + whole) % AZ], relay_roll[c, (d + whole + 1) % AZ])
+                    small < NY - part, relay_roll[c, (d + whole) & (AZ - 1)], relay_roll[c, (d + whole + 1) & (AZ - 1)])
 
             arrived(0)
             turn((0,), (0,), shift_0)
-
-            def near_step(k, carry):
-                d = peer(k, True)
+            for d in range(AZ):
                 near_out[d] = pick(0, d, shift_0)
+            for d, _ in peers(True):
                 pltpu.make_async_remote_copy(
                     near_out.at[d], ghost.at[0, side, f, j, rows], b_send, x_recv.at[0, side],
                     device_id=(d, across), device_id_type=MESH).start()
-                return carry
-
-            lax.fori_loop(0, AZ, near_step, 0, unroll=4)
+
             turn((0,), (0,), shift_1)
+            for d in range(AZ):
+                far_out[d, 0:8] = pick(0, d, shift_1)
+            sub = lax.broadcasted_iota(jnp.int32, (8, NY), 0)
+            for d in range(AZ):
+                ends = jnp.where(small < NY // 2, far_out[(d + 1) % AZ, 0:8], far_out[(d + AZ - 1) % AZ, 0:8])
+                ends = jnp.where(small < 4, pltpu.roll(ends, 2, 1), 0.0)
+                for width in (4, 8, 16):
+                    ends = ends + pltpu.roll(ends, width, 1)
+                ends = jnp.where(small >> 2 == 7 - sub, ends, 0.0)
+                far_out[d, 16:17] = jnp.sum(ends, axis=0, keepdims=True)
             arrived(1)
             turn((1,), (1,), shift_1)
-
-            def pick_step(d, carry):
-                for t in range(2):
-                    far_out[d, t] = pick(t, d, shift_1)
-                return carry
-
-            lax.fori_loop(0, AZ, pick_step, 0, unroll=8)
-
-            def far_step(k, carry):
-                d = peer(k, True)
-                far_out[d, 2] = jnp.where(small < NY // 2, far_out[(d + 1) % AZ, 0], far_out[(d + AZ - 1) % AZ, 0])
+            for d in range(AZ):
+                far_out[d, 8:16] = pick(1, d, shift_1)
+            piece = far_in.at[az, pl.ds(0, 17)]
+            for d, _ in peers(True):
                 pltpu.make_async_remote_copy(
-                    far_out.at[d], far_in.at[:, f, j, rows], far_send, far_recv,
+                    far_out.at[d, pl.ds(0, 17)], piece, far_send, far_recv,
                     device_id=(d, across), device_id_type=MESH).start()
-                return carry
-
-            lax.fori_loop(0, AZ, far_step, 0, unroll=4)
+
             shift_2 = (shift_0 - shift_1 + COLS) % COLS
             turn((0,), (0,), shift_2)
 
-            def plane_step(d, carry):
+            for d in range(AZ):
                 plane_out[d] = pick(0, d, shift_2)
-                return carry
-
-            lax.fori_loop(0, AZ, plane_step, 0, unroll=8)
-
-            def send(d):
+
+            def send(d, plane):
                 pltpu.make_async_remote_copy(
                     plane_out.at[d], plane_in.at[f, j, rows], plane_send, plane_recv,
                     device_id=(d, RAD - 1 - across), device_id_type=MESH).start()
@@ -386,13 +386,15 @@
 
     def sheared_rows(w):
         pltpu.make_async_copy(plane_in, plane_in, plane_recv).wait()
-        pltpu.make_async_copy(far_in, far_in, far_recv).wait()
+        whole = far_in.at[:, pl.ds(0, 17)]
+        pltpu.make_async_copy(whole, whole, far_recv).wait()
         far_at = jnp.where(rad == 0, 0, 4)
         plane_kick = jnp.where(rad == 0, -shear_jump, shear_jump)
         for f in range(NF):
             for j in range(2):
-                ext_rows[f, 2 + j] = far_in[0, f, j]
-                ext_rows[f, far_at + j] = far_in[1, f, j]
+                at = f * 4 + j * 2
+                ext_rows[f, 2 + j] = far_in[at:at + 2, 0:8].reshape(NZ, NY)
+                ext_rows[f, far_at + j] = far_in[at:at + 2, 8:16].reshape(NZ, NY)
                 value = plane_in[f, j]
                 if f == 2:
                     value = value + plane_kick
@@ -403,7 +405,12 @@
         for j in range(2):
             cells = [ext_rows[f, 2 + j] for f in range(NF)]
             flux = rolled_faces(cells, 0, 2)
-            part = ghosted_divergence(cells, [far_in[2, f, j] for f in range(NF)], lane, 1)
+            columns = []
+            for f in range(NF):
+                pair = [pltpu.roll(jnp.broadcast_to(far_in[f * 4 + j * 2 + half, 16:17], (8, NY)), NY - 30, 1,
+                                   stride=4, stride_axis=0) for half in range(2)]
+                columns.append(jnp.concatenate(pair, axis=0))
+            part = ghosted_divergence(cells, columns, lane, 1)
             u = conserved_of(cells)
             for f in range(NF):
                 total = pltpu.roll(flux[f], NZ - 1, 0) - flux[f] + part[f] + (ext_flux[f, j + 1] - ext_flux[f, j])
@@ -444,8 +451,8 @@
         y_part()
         x_faces(w, fx, 2, 7)
 
+    start_y(0)
     scatter()
-    start_y(0)
     bulk(w1)
     finish_y(0)
     lax.fori_loop(2, 6, middle, 0)
@@ -511,7 +518,8 @@
     @pl.when(relay)
     def _():
         pltpu.make_async_copy(near_out, near_out, b_send).wait()
-        pltpu.make_async_copy(far_out, far_out, far_send).wait()
+        sent = far_out.at[:, pl.ds(0, 17)]
+        pltpu.make_async_copy(sent, sent, far_send).wait()
         most = plane_out.at[pl.ds(0, AZ - 1)]
         pltpu.make_async_copy(most, most, plane_send).wait()
 
@@ -543,9 +551,9 @@
             pltpu.VMEM((2, AZ, 8, NY), f32),
             pltpu.VMEM((2, AZ, 8, NY), f32),
             pltpu.VMEM((AZ, 8, NY), f32),
-            pltpu.VMEM((AZ, 3, 8, NY), f32),
+            pltpu.VMEM((AZ, 24, NY), f32),
             pltpu.VMEM((AZ, 8, NY), f32),
-            pltpu.VMEM((3, NF, 2, NZ, NY), f32),
+            pltpu.VMEM((AZ, 24, NY), f32),
             pltpu.VMEM((NF, 2, NZ, NY), f32),
             pltpu.VMEM((NF, 6, NZ, NY), f32),
             pltpu.VMEM((NF, 3, NZ, NY), f32),

time: 37.8 us -> 34.8 us (0.921)
  Pallas kernels: 36.2 us -> 33.2 us
    pallas_call x1, Pallas kernels: 36.2 us -> 33.2 us  [shards(): pl.pallas_call(kernel, out_shape=jax.ShapeDtypeStruct((NF, NZ, NX, NY), f...]
where the time goes in v5:
time: 34.8 us; the launch traced here: 34.7 us
  Pallas kernels  33.2 us (95%)
  local copies, waits for them, and re-layouts  1.45 us (4%)
    pallas_call x1, Pallas kernels, shards(): pl.pallas_call(kernel, out_shape=jax.ShapeDtypeStruct((NF, NZ, NX, NY), f...  33.2 us
    unnamed x3, local copies, waits for them, and re-layouts  1.45 us

profile of v5, /device:TPU:1, one launch (start us, length us, event | category | flops | bytes accessed | tf_op | source)
XLA Modules:
  0.0 34.7 jit_solution(12612754040697786691)
XLA Ops:
  0.0 0.0 copy-start
  0.0 0.7 %copy-done = s32[2]{0:T(128)S(1)} copy-done((s32[2]{0:T(128)S(1)}, s32[2]{0:T(128)}, u32[]{:S(2)}) %copy-start) | copy-done | bytes 32
  0.7 33.2 %mhd_step.1 = f32[8,16,8,128]{3,2,1,0:T(8,128)S(1)} custom-call(s32[2]{0:T(128)S(1)} %copy-done, f32[8,16,8,128]{3,2,1,0:T(8,128)} %u_hbm.1), custom_call_target="tpu_custom_call" | custom-call | tf_op jit(solution)/shard_map/mhd_step/pallas_call | solution.py:533
  33.9 0.8 %copy.4 = f32[8,16,8,128]{3,2,1,0:T(8,128)} copy(f32[8,16,8,128]{3,2,1,0:T(8,128)S(1)} %mhd_step.1) | data formatting | bytes 1048576
Async XLA Ops:
  0.0 0.7 %copy-start = (s32[2]{0:T(128)S(1)}, s32[2]{0:T(128)}, u32[]{:S(2)}) copy-start(s32[2]{0:T(128)} %shift_hbm.1) | copy-start | bytes 28

commit v6 on v5

--- a/solution.py
+++ b/solution.py
@@ -133,7 +133,7 @@
 
     def peers(across):
         out = []
-        for z in reversed(z_list) if across else z_list:
+        for z in range(4) if across else z_list:
             for x in x_list:
                 for core in core_list:
                     out.append((z * 8 + x * 2 + core, plane_of(z, x, core)))
@@ -575,7 +575,8 @@
         name="mhd_step",
         compiler_params=pltpu.CompilerParams(
             collective_id=0, has_side_effects=True, vmem_limit_bytes=53 * 1024 * 1024),
-    )(shear_shift, conserved)
+    )(pltpu.with_memory_space_constraint(shear_shift, pltpu.HBM),
+      pltpu.with_memory_space_constraint(conserved, pltpu.HBM))
 
 
 def solution(mesh):

time: 34.8 us -> 33.8 us (0.971)
  local copies, waits for them, and re-layouts: 1.45 us -> 0.8 us
    unnamed x3 -> x1, local copies, waits for them, and re-layouts: 1.45 us -> 0.8 us
where the time goes in v6:
time: 33.8 us; the launch traced here: 33.7 us
  Pallas kernels  32.9 us (97%)
  local copies, waits for them, and re-layouts  0.8 us (2%)
    pallas_call x1, Pallas kernels, shards(): pl.pallas_call(kernel, out_shape=jax.ShapeDtypeStruct((NF, NZ, NX, NY), f...  32.9 us
    unnamed x1, local copies, waits for them, and re-layouts  0.8 us

profile of v6, /device:TPU:1, one launch (start us, length us, event | category | flops | bytes accessed | tf_op | source)
XLA Modules:
  0.0 33.7 jit_solution(14531006714099449548)
XLA Ops:
  0.0 32.9 %mhd_step.1 = f32[8,16,8,128]{3,2,1,0:T(8,128)S(1)} custom-call(s32[2]{0:T(128)} %shift_hbm.1, f32[8,16,8,128]{3,2,1,0:T(8,128)} %u_hbm.1), custom_call_target="tpu_custom_call" | custom-call | tf_op jit(solution)/shard_map/mhd_step/pallas_call | solution.py:533
  32.9 0.8 %copy.4 = f32[8,16,8,128]{3,2,1,0:T(8,128)} copy(f32[8,16,8,128]{3,2,1,0:T(8,128)S(1)} %mhd_step.1) | data formatting | bytes 1048576

commit v7 on v6

--- a/solution.py
+++ b/solution.py
@@ -104,7 +104,7 @@
 
 
 def kernel(shift_hbm, u_hbm, out_ref, raw, w1, w2, acc, fx, tend, wt, ft, y_out, y_in, ghost, stage, relay_in,
-           relay_roll, near_out, far_out, plane_out, far_in, plane_in, ext_rows, ext_flux, shift_ref, in_sem, shift_sem,
+           relay_roll, near_out, far_out, plane_out, far_in, plane_in, ext_rows, ext_flux, ext_part, shift_ref, in_sem, shift_sem,
            x_send, x_recv, y_send, y_recv, a_send, a_recv, b_send, far_send, far_recv, plane_send, plane_recv):
     az = lax.axis_index("az")
     rad = lax.axis_index("rad")
@@ -292,17 +292,20 @@
                 for width in (4, 8, 16):
                     ends = ends + pltpu.roll(ends, width, 1)
                 ends = jnp.where(small >> 2 == 7 - sub, ends, 0.0)
-                far_out[d, 16:17] = jnp.sum(ends, axis=0, keepdims=True)
+                far_out[d, 8:9] = jnp.sum(ends, axis=0, keepdims=True)
+
+            def answer(begin, rows, t):
+                for d, _ in peers(True):
+                    pltpu.make_async_remote_copy(
+                        far_out.at[d, pl.ds(begin, rows)], far_in.at[az, pl.ds(begin, rows)],
+                        far_send.at[t], far_recv.at[t], device_id=(d, across), device_id_type=MESH).start()
+
+            answer(0, 9, 0)
             arrived(1)
             turn((1,), (1,), shift_1)
             for d in range(AZ):
-                far_out[d, 8:16] = pick(1, d, shift_1)
-            piece = far_in.at[az, pl.ds(0, 17)]
-            for d, _ in peers(True):
-                pltpu.make_async_remote_copy(
-                    far_out.at[d, pl.ds(0, 17)], piece, far_send, far_recv,
-                    device_id=(d, across), device_id_type=MESH).start()
-
+                far_out[d, 16:24] = pick(1, d, shift_1)
+            answer(16, 8, 1)
             shift_2 = (shift_0 - shift_1 + COLS) % COLS
             turn((0,), (0,), shift_2)
 
@@ -384,36 +387,43 @@
                 value = ghost[sec, side, f, j]
                 w[f, 10 * side + j] = value + kick if f == 2 else value
 
+    def sheared_near():
+        near = far_in.at[:, pl.ds(0, 9)]
+        pltpu.make_async_copy(near, near, far_recv.at[0]).wait()
+        for j in range(2):
+            cells, columns = [], []
+            for f in range(NF):
+                at = f * 4 + j * 2
+                cells.append(far_in[at:at + 2, 0:8].reshape(NZ, NY))
+                pair = [pltpu.roll(jnp.broadcast_to(far_in[at + half, 8:9], (8, NY)), NY - 30, 1,
+                                   stride=4, stride_axis=0) for half in range(2)]
+                columns.append(jnp.concatenate(pair, axis=0))
+                ext_rows[f, 2 + j] = cells[f]
+            flux = rolled_faces(cells, 0, 2)
+            part = ghosted_divergence(cells, columns, lane, 1)
+            for f in range(NF):
+                ext_part[f, j] = pltpu.roll(flux[f], NZ - 1, 0) - flux[f] + part[f]
+
     def sheared_rows(w):
         pltpu.make_async_copy(plane_in, plane_in, plane_recv).wait()
-        whole = far_in.at[:, pl.ds(0, 17)]
-        pltpu.make_async_copy(whole, whole, far_recv).wait()
+        far = far_in.at[:, pl.ds(16, 8)]
+        pltpu.make_async_copy(far, far, far_recv.at[1]).wait()
         far_at = jnp.where(rad == 0, 0, 4)
         plane_kick = jnp.where(rad == 0, -shear_jump, shear_jump)
         for f in range(NF):
             for j in range(2):
                 at = f * 4 + j * 2
-                ext_rows[f, 2 + j] = far_in[at:at + 2, 0:8].reshape(NZ, NY)
-                ext_rows[f, far_at + j] = far_in[at:at + 2, 8:16].reshape(NZ, NY)
+                ext_rows[f, far_at + j] = far_in[at:at + 2, 16:24].reshape(NZ, NY)
                 value = plane_in[f, j]
                 if f == 2:
                     value = value + plane_kick
                 ext_rows[f, 4 - far_at + j] = value
         x_faces(ext_rows, ext_flux, 0, 3)
-
         at = jnp.where(rad == 0, 0, 10)
         for j in range(2):
-            cells = [ext_rows[f, 2 + j] for f in range(NF)]
-            flux = rolled_faces(cells, 0, 2)
-            columns = []
+            u = conserved_of([ext_rows[f, 2 + j] for f in range(NF)])
             for f in range(NF):
-                pair = [pltpu.roll(jnp.broadcast_to(far_in[f * 4 + j * 2 + half, 16:17], (8, NY)), NY - 30, 1,
-                                   stride=4, stride_axis=0) for half in range(2)]
-                columns.append(jnp.concatenate(pair, axis=0))
-            part = ghosted_divergence(cells, columns, lane, 1)
-            u = conserved_of(cells)
-            for f in range(NF):
-                total = pltpu.roll(flux[f], NZ - 1, 0) - flux[f] + part[f] + (ext_flux[f, j + 1] - ext_flux[f, j])
+                total = ext_part[f, j] + (ext_flux[f, j + 1] - ext_flux[f, j])
                 u[f] = u[f] - (0.5 * time_step) * total
             mid = primitive_of(u)
             mid[2] = mid[2] - plane_kick
@@ -480,6 +490,7 @@
 
         @pl.when(sheared)
         def _():
+            sheared_near()
             sheared_rows(w2)
 
         @pl.when(jnp.logical_not(sheared))
@@ -518,8 +529,9 @@
     @pl.when(relay)
     def _():
         pltpu.make_async_copy(near_out, near_out, b_send).wait()
-        sent = far_out.at[:, pl.ds(0, 17)]
-        pltpu.make_async_copy(sent, sent, far_send).wait()
+        for t, begin, rows in ((0, 0, 9), (1, 16, 8)):
+            sent = far_out.at[:, pl.ds(begin, rows)]
+            pltpu.make_async_copy(sent, sent, far_send.at[t]).wait()
         most = plane_out.at[pl.ds(0, AZ - 1)]
         pltpu.make_async_copy(most, most, plane_send).wait()
 
@@ -557,6 +569,7 @@
             pltpu.VMEM((NF, 2, NZ, NY), f32),
             pltpu.VMEM((NF, 6, NZ, NY), f32),
             pltpu.VMEM((NF, 3, NZ, NY), f32),
+            pltpu.VMEM((NF, 2, NZ, NY), f32),
             pltpu.SMEM((2,), jnp.int32),
             pltpu.SemaphoreType.DMA,
             pltpu.SemaphoreType.DMA,
@@ -567,8 +580,8 @@
             pltpu.SemaphoreType.DMA((2,)),
             pltpu.SemaphoreType.DMA((2,)),
             pltpu.SemaphoreType.DMA,
-            pltpu.SemaphoreType.DMA,
-            pltpu.SemaphoreType.DMA,
+            pltpu.SemaphoreType.DMA((2,)),
+            pltpu.SemaphoreType.DMA((2,)),
             pltpu.SemaphoreType.DMA,
             pltpu.SemaphoreType.DMA,
         ],

time: 33.8 us -> 33.2 us (0.982); the launches traced: 33.7 us -> 32.6 us
  Pallas kernels: 32.9 us -> 31.8 us
    pallas_call x1, Pallas kernels: 32.9 us -> 31.8 us  [shards(): pl.pallas_call(kernel, out_shape=jax.ShapeDtypeStruct((NF, NZ, NX, NY), f...]
where the time goes in v7:
time: 33.2 us; the launch traced here: 32.6 us
  Pallas kernels  31.8 us (96%)
  local copies, waits for them, and re-layouts  0.8 us (2%)
    pallas_call x1, Pallas kernels, shards(): pl.pallas_call(kernel, out_shape=jax.ShapeDtypeStruct((NF, NZ, NX, NY), f...  31.8 us
    unnamed x1, local copies, waits for them, and re-layouts  0.8 us

profile of v7, /device:TPU:1, one launch (start us, length us, event | category | flops | bytes accessed | tf_op | source)
XLA Modules:
  0.0 32.6 jit_solution(14299517158261402657)
XLA Ops:
  0.0 31.8 %mhd_step.1 = f32[8,16,8,128]{3,2,1,0:T(8,128)S(1)} custom-call(s32[2]{0:T(128)} %shift_hbm.1, f32[8,16,8,128]{3,2,1,0:T(8,128)} %u_hbm.1), custom_call_target="tpu_custom_call" | custom-call | tf_op jit(solution)/shard_map/mhd_step/pallas_call | solution.py:545
  31.8 0.8 %copy.4 = f32[8,16,8,128]{3,2,1,0:T(8,128)} copy(f32[8,16,8,128]{3,2,1,0:T(8,128)S(1)} %mhd_step.1) | data formatting | bytes 1048576

commit v8 on v7

--- a/solution.py
+++ b/solution.py
@@ -323,14 +323,14 @@
             def _():
                 pltpu.make_async_copy(plane_out.at[az], plane_in.at[f, j, rows], plane_recv).start()
 
-    def z_part(w):
-        def row(x, carry):
-            flux = rolled_faces([w[f, x + 2] for f in range(NF)], 0, 2)
-            for f in range(NF):
-                acc[f, x] = pltpu.roll(flux[f], NZ - 1, 0) - flux[f]
-            return carry
-
-        lax.fori_loop(0, NX, row, 0)
+    def z_row(w, x):
+        flux = rolled_faces([w[f, x + 2] for f in range(NF)], 0, 2)
+        for f in range(NF):
+            acc[f, x] = pltpu.roll(flux[f], NZ - 1, 0) - flux[f]
+
+    def z_first(x, carry):
+        z_row(w1, x)
+        return carry
 
     def y_faces(k):
         lefts, rights = [], []
@@ -446,6 +446,7 @@
         for f in range(NF):
             tend[f, x] = total[f]
             w2[f, x + 2] = w[f]
+        z_row(w2, x)
         return carry
 
     out_rows = out_ref.reshape(NF * NZ * NX, NY)
@@ -456,14 +457,11 @@
             out_rows[pl.ds(f * NZ * NX + x, NZ, NX), :] = 0.5 * (tend[f, x] + total[f])
         return carry
 
-    def bulk(w):
-        z_part(w)
-        y_part()
-        x_faces(w, fx, 2, 7)
-
     start_y(0)
     scatter()
-    bulk(w1)
+    lax.fori_loop(0, NX, z_first, 0)
+    y_part()
+    x_faces(w1, fx, 2, 7)
     finish_y(0)
     lax.fori_loop(2, 6, middle, 0)
     start_x(0, w1, 0)
@@ -477,12 +475,20 @@
         side_faces(w1, side)
         lax.fori_loop(6 * side, 6 * side + 2, middle, 0)
         start_x(1, w2, side)
+
+        @pl.when(k == 0)
+        def _():
+            soon = jnp.where(rad == 0, 4, 2)
+            x_faces(w2, fx, soon, soon + 3)
+
         return carry
 
     lax.fori_loop(0, 2, first_side, 0)
     turn_y(1, w2)
     start_y(1)
-    bulk(w2)
+    y_part()
+    late = jnp.where(rad == 0, 2, 5)
+    x_faces(w2, fx, late, late + 2)
 
     def second_side(k, carry):
         side = side_at(k)

time: 33.2 us -> 32.7 us (0.985); the launches traced: 32.6 us -> 32.6 us
  no operation moved by 1% of the time
where the time goes in v8:
time: 32.7 us; the launch traced here: 32.6 us
  Pallas kernels  31.8 us (97%)
  local copies, waits for them, and re-layouts  0.8 us (2%)
    pallas_call x1, Pallas kernels, shards(): pl.pallas_call(kernel, out_shape=jax.ShapeDtypeStruct((NF, NZ, NX, NY), f...  31.8 us
    unnamed x1, local copies, waits for them, and re-layouts  0.8 us

profile of v8, /device:TPU:1, one launch (start us, length us, event | category | flops | bytes accessed | tf_op | source)
XLA Modules:
  0.0 32.6 jit_solution(6816168268964806176)
XLA Ops:
  0.0 31.8 %mhd_step.1 = f32[8,16,8,128]{3,2,1,0:T(8,128)S(1)} custom-call(s32[2]{0:T(128)} %shift_hbm.1, f32[8,16,8,128]{3,2,1,0:T(8,128)} %u_hbm.1), custom_call_target="tpu_custom_call" | custom-call | tf_op jit(solution)/shard_map/mhd_step/pallas_call | solution.py:551
  31.8 0.8 %copy.4 = f32[8,16,8,128]{3,2,1,0:T(8,128)} copy(f32[8,16,8,128]{3,2,1,0:T(8,128)S(1)} %mhd_step.1) | data formatting | bytes 1048576

commit v9 on v8

--- a/solution.py
+++ b/solution.py
@@ -216,21 +216,20 @@
             y_out.at[sec, side], y_in.at[sec, side], y_send.at[sec, side], y_recv.at[sec, side],
             device_id=(right if up else left, rad), device_id_type=MESH)
 
-    def scatter():
+    def scatter(t):
         @pl.when(edge)
         def _():
             base, sign = jnp.where(rad == 0, 3, 4), jnp.where(rad == 0, -1, 1)
-            for t in range(2):
-                def send(p, plane):
-                    pltpu.make_async_remote_copy(
-                        stage.at[t, p], relay_in.at[t, az], a_send.at[t], a_recv.at[t],
-                        device_id=(p, base + sign * plane), device_id_type=MESH).start()
-
-                others(send)
-
-                @pl.when(both)
-                def _():
-                    pltpu.make_async_copy(stage.at[t, az], relay_in.at[t, az], a_recv.at[t]).start()
+            def send(p, plane):
+                pltpu.make_async_remote_copy(
+                    stage.at[t, p], relay_in.at[t, az], a_send.at[t], a_recv.at[t],
+                    device_id=(p, base + sign * plane), device_id_type=MESH).start()
+
+            others(send)
+
+            @pl.when(both)
+            def _():
+                pltpu.make_async_copy(stage.at[t, az], relay_in.at[t, az], a_recv.at[t]).start()
 
     def start_x(sec, w, side):
         @pl.when((side == 1) & (rad < RAD - 1))
@@ -275,9 +274,8 @@
 
             arrived(0)
             turn((0,), (0,), shift_0)
-            for d in range(AZ):
+            for d, _ in peers(True):
                 near_out[d] = pick(0, d, shift_0)
-            for d, _ in peers(True):
                 pltpu.make_async_remote_copy(
                     near_out.at[d], ghost.at[0, side, f, j, rows], b_send, x_recv.at[0, side],
                     device_id=(d, across), device_id_type=MESH).start()
@@ -351,7 +349,7 @@
 
         lax.fori_loop(0, 7, pair, 0)
 
-    def x_faces(w, flux_ref, begin, end):
+    def x_faces(w, flux_ref, begin, end, unrolled=0):
         def face(i, carry):
             lefts, rights = [], []
             for f in range(NF):
@@ -364,7 +362,11 @@
                 flux_ref[f, i] = flux[f]
             return carry
 
-        lax.fori_loop(begin, end, face, 0)
+        if unrolled:
+            for k in range(unrolled):
+                face(begin + k, 0)
+        else:
+            lax.fori_loop(begin, end, face, 0)
 
     def finish_y(sec):
         y_copy(sec, True).wait_recv()
@@ -418,7 +420,7 @@
                 if f == 2:
                     value = value + plane_kick
                 ext_rows[f, 4 - far_at + j] = value
-        x_faces(ext_rows, ext_flux, 0, 3)
+        x_faces(ext_rows, ext_flux, 0, 3, 3)
         at = jnp.where(rad == 0, 0, 10)
         for j in range(2):
             u = conserved_of([ext_rows[f, 2 + j] for f in range(NF)])
@@ -434,7 +436,7 @@
         return (k + jnp.where(rad == 0, 1, 0)) % 2
 
     def side_faces(w, side):
-        x_faces(w, fx, 7 * side, 7 * side + 2)
+        x_faces(w, fx, 7 * side, 7 * side + 2, 2)
 
     def row_total(x):
         return [-0.5 * (acc[f, x] + (fx[f, x + 1] - fx[f, x])) for f in range(NF)]
@@ -446,6 +448,9 @@
         for f in range(NF):
             tend[f, x] = total[f]
             w2[f, x + 2] = w[f]
+        return carry
+
+    def z_second(x, carry):
         z_row(w2, x)
         return carry
 
@@ -458,12 +463,14 @@
         return carry
 
     start_y(0)
-    scatter()
+    scatter(0)
     lax.fori_loop(0, NX, z_first, 0)
     y_part()
     x_faces(w1, fx, 2, 7)
+    scatter(1)
     finish_y(0)
     lax.fori_loop(2, 6, middle, 0)
+    lax.fori_loop(2, 6, z_second, 0)
     start_x(0, w1, 0)
     start_x(0, w1, 1)
     load_shift.wait()
@@ -478,6 +485,7 @@
 
         @pl.when(k == 0)
         def _():
+            lax.fori_loop(6 * side, 6 * side + 2, z_second, 0)
             soon = jnp.where(rad == 0, 4, 2)
             x_faces(w2, fx, soon, soon + 3)
 
@@ -486,6 +494,8 @@
     lax.fori_loop(0, 2, first_side, 0)
     turn_y(1, w2)
     start_y(1)
+    after = 6 * side_at(1)
+    lax.fori_loop(after, after + 2, z_second, 0)
     y_part()
     late = jnp.where(rad == 0, 2, 5)
     x_faces(w2, fx, late, late + 2)
@@ -496,7 +506,6 @@
 
         @pl.when(sheared)
         def _():
-            sheared_near()
             sheared_rows(w2)
 
         @pl.when(jnp.logical_not(sheared))
@@ -504,10 +513,18 @@
             receive_side(1, w2, side)
 
         side_faces(w2, side)
+
+        @pl.when(k == 0)
+        def _():
+            @pl.when(edge)
+            def _():
+                sheared_near()
+
+            finish_y(1)
+
         return carry
 
     lax.fori_loop(0, 2, second_side, 0)
-    finish_y(1)
     lax.fori_loop(0, NX, last, 0)
 
     for sec, w in ((0, w1), (1, w2)):

time: 32.7 us -> 32.8 us (level)
  no operation moved by 1% of the time
where the time goes in v9:
time: 32.8 us; the launch traced here: 32.4 us
  Pallas kernels  31.6 us (96%)
  local copies, waits for them, and re-layouts  0.8 us (2%)
    pallas_call x1, Pallas kernels, shards(): pl.pallas_call(kernel, out_shape=jax.ShapeDtypeStruct((NF, NZ, NX, NY), f...  31.6 us
    unnamed x1, local copies, waits for them, and re-layouts  0.8 us

profile of v9, /device:TPU:1, one launch (start us, length us, event | category | flops | bytes accessed | tf_op | source)
XLA Modules:
  0.0 32.4 jit_solution(15904224486403597644)
XLA Ops:
  0.0 31.6 %mhd_step.1 = f32[8,16,8,128]{3,2,1,0:T(8,128)S(1)} custom-call(s32[2]{0:T(128)} %shift_hbm.1, f32[8,16,8,128]{3,2,1,0:T(8,128)} %u_hbm.1), custom_call_target="tpu_custom_call" | custom-call | tf_op jit(solution)/shard_map/mhd_step/pallas_call | solution.py:568
  31.6 0.8 %copy.4 = f32[8,16,8,128]{3,2,1,0:T(8,128)} copy(f32[8,16,8,128]{3,2,1,0:T(8,128)S(1)} %mhd_step.1) | data formatting | bytes 1048576

commit v10 on v8

--- a/solution.py
+++ b/solution.py
@@ -216,21 +216,20 @@
             y_out.at[sec, side], y_in.at[sec, side], y_send.at[sec, side], y_recv.at[sec, side],
             device_id=(right if up else left, rad), device_id_type=MESH)
 
-    def scatter():
+    def scatter(t):
         @pl.when(edge)
         def _():
             base, sign = jnp.where(rad == 0, 3, 4), jnp.where(rad == 0, -1, 1)
-            for t in range(2):
-                def send(p, plane):
-                    pltpu.make_async_remote_copy(
-                        stage.at[t, p], relay_in.at[t, az], a_send.at[t], a_recv.at[t],
-                        device_id=(p, base + sign * plane), device_id_type=MESH).start()
-
-                others(send)
-
-                @pl.when(both)
-                def _():
-                    pltpu.make_async_copy(stage.at[t, az], relay_in.at[t, az], a_recv.at[t]).start()
+            def send(p, plane):
+                pltpu.make_async_remote_copy(
+                    stage.at[t, p], relay_in.at[t, az], a_send.at[t], a_recv.at[t],
+                    device_id=(p, base + sign * plane), device_id_type=MESH).start()
+
+            others(send)
+
+            @pl.when(both)
+            def _():
+                pltpu.make_async_copy(stage.at[t, az], relay_in.at[t, az], a_recv.at[t]).start()
 
     def start_x(sec, w, side):
         @pl.when((side == 1) & (rad < RAD - 1))
@@ -458,10 +457,11 @@
         return carry
 
     start_y(0)
-    scatter()
+    scatter(0)
     lax.fori_loop(0, NX, z_first, 0)
     y_part()
     x_faces(w1, fx, 2, 7)
+    scatter(1)
     finish_y(0)
     lax.fori_loop(2, 6, middle, 0)
     start_x(0, w1, 0)

time: 32.7 us -> 32.6 us (level)
  no operation moved by 1% of the time
where the time goes in v10:
time: 32.6 us; the launch traced here: 32.5 us
  Pallas kernels  31.7 us (97%)
  local copies, waits for them, and re-layouts  0.8 us (2%)
    pallas_call x1, Pallas kernels, shards(): pl.pallas_call(kernel, out_shape=jax.ShapeDtypeStruct((NF, NZ, NX, NY), f...  31.7 us
    unnamed x1, local copies, waits for them, and re-layouts  0.8 us

profile of v10, /device:TPU:1, one launch (start us, length us, event | category | flops | bytes accessed | tf_op | source)
XLA Modules:
  0.0 32.5 jit_solution(11973644362705558371)
XLA Ops:
  0.0 31.7 %mhd_step.1 = f32[8,16,8,128]{3,2,1,0:T(8,128)S(1)} custom-call(s32[2]{0:T(128)} %shift_hbm.1, f32[8,16,8,128]{3,2,1,0:T(8,128)} %u_hbm.1), custom_call_target="tpu_custom_call" | custom-call | tf_op jit(solution)/shard_map/mhd_step/pallas_call | solution.py:551
  31.7 0.8 %copy.4 = f32[8,16,8,128]{3,2,1,0:T(8,128)} copy(f32[8,16,8,128]{3,2,1,0:T(8,128)S(1)} %mhd_step.1) | data formatting | bytes 1048576
